TPU v7x, 32 devices: a whole 2x2x4 slice. The times are simulated.
32 devices in a mesh: section: 4 (over y, x), batch: 8 (over z, core).
Axes of the slice: x: 2, y: 2, z: 4, core: 2. Of those that a mesh axis runs over, the one named last changes fastest.
Arguments:
- inputs: bfloat16 [2, 6144, 768], P(None, 'batch', 'section'), may hold values from -6 to 6
- in_weight: float32 [4, 768, 3072], P('section')
- down_weight: float32 [6144, 768], P('section'), may hold values from -0.109375 to 0.109375
- out_bias: float32 [4, 768], P('section'), may hold values from -3 to 3
- norm_gains: float32 [4, 768], P('section'), may hold values from 0.5 to 1.5
- norm_shifts: float32 [4, 768], P('section'), may hold values from -2 to 2
- projection: float32 [768, 128], P(None, 'section'), may hold values from -0.21875 to 0.21875
- passage_lengths: int32 [2, 8, 3], P(None, 'batch'), may hold values from 1 to 512, 640 in all within a row
- positive: int32 [2, 32], P(None, 'batch'), may hold values from 0 to 2
Outputs:
- total_loss: float32 [], replicated
- input_grad: float32 [2, 6144, 768], P(None, 'batch', 'section')
- in_weight_grad: float32 [4, 768, 3072], P('section')
- down_weight_grad: float32 [6144, 768], P('section')
- out_bias_grad: float32 [4, 768], P('section')
- norm_gain_grad: float32 [4, 768], P('section')
- norm_shift_grad: float32 [4, 768], P('section')
- projection_grad: float32 [768, 128], P(None, 'section')
Inputs may be any that keep to these rules, and one draw needn't show every extreme that they name: `passage_lengths`: passage lengths of one micro-batch on one batch device sum to 640; one of them is 512.
All inputs are finite; a program needn't handle non-finite values.
Results may differ from a plain program's by a relative error of at most 0.018.
Values may be sent and summed in bfloat16 or wider, within the bound.
A program may use at most 256 MiB of HBM per device.

v0:
```python
from functools import partial

import jax
import jax.numpy as jnp
from jax import lax
from jax.sharding import PartitionSpec as P

D = 768
HEADS = 12
FF = 3072
QUERY_LENGTH = 32
QUERY_COUNT = 4
PASSAGE_TOKENS = 640


SOFTMAX_DIVISOR = 0.1
SIMILARITY_SCALE = 0.25
NORM_EPSILON = 1e-06


def from_behind(block, axis, distance):
    devices = range(lax.axis_size(axis))
    route = [(i - distance, i) for i in devices if i - distance in devices]
    return lax.ppermute(block, axis, route)


def shortened(value):

    def short(part):
        return part.astype(jnp.bfloat16) if part.dtype == jnp.float32 else part

    return jax.tree.map(short, value)


def layer_norm(residual, gain, shift):
    row_mean = jnp.mean(residual, -1, keepdims=True)
    centered = residual - row_mean
    return (
        centered * lax.rsqrt(jnp.mean(centered * centered, -1, keepdims=True) + NORM_EPSILON) * gain
        + shift
    )


def normalize(projected):
    return projected * lax.rsqrt(jnp.sum(projected * projected, -1, keepdims=True) + NORM_EPSILON)


def exact_gelu(values):
    return jax.nn.gelu(values, approximate=False)


def sequence_masks(lengths):
    segment_ends = jnp.cumsum(lengths)
    starts = segment_ends - lengths
    token_positions = jnp.arange(PASSAGE_TOKENS, dtype=jnp.int32)
    document_word_validity = (token_positions[None, :] >= starts[:, None]) & (
        token_positions[None, :] < segment_ends[:, None]
    )
    passage_token_ids = (
        jnp.sum((token_positions[:, None] >= segment_ends[None, :]).astype(jnp.int32), 1)
        + QUERY_COUNT
    )
    query_token_ids = jnp.arange(QUERY_COUNT * QUERY_LENGTH, dtype=jnp.int32) // QUERY_LENGTH
    sequence_ids = jnp.concatenate([query_token_ids, passage_token_ids])
    return (document_word_validity, sequence_ids[:, None] == sequence_ids[None, :])


def maxsim_loss(word_pair_affinity, document_word_validity, positive):
    divided_logit_matrix = jnp.where(
        document_word_validity[None, :, :],
        word_pair_affinity[:, None, :] / SOFTMAX_DIVISOR,
        -1000000000.0,
    )
    softened_largest_value = SOFTMAX_DIVISOR * jax.nn.logsumexp(divided_logit_matrix, -1)
    passage_scores = (
        jnp.sum(softened_largest_value.reshape(QUERY_COUNT, QUERY_LENGTH, -1), 1) * SIMILARITY_SCALE
    )
    choose = jnp.arange(passage_scores.shape[1], dtype=jnp.int32)[None, :] == positive[:, None]
    picked = jnp.sum(jnp.where(choose, passage_scores, 0.0), 1)
    return jnp.sum(jax.nn.logsumexp(passage_scores, -1) - picked)


def attention_parts(encoder_part_entry, weight_in, same_sequence):
    head_dim = D // HEADS
    row_total_count = encoder_part_entry.shape[0]
    projected = jnp.dot(
        encoder_part_entry, weight_in[:, : 3 * D], preferred_element_type=jnp.float32
    )
    queries = projected[:, :D].astype(jnp.bfloat16).reshape(row_total_count, HEADS, head_dim)
    keys = projected[:, D : 2 * D].astype(jnp.bfloat16).reshape(row_total_count, HEADS, head_dim)
    values = projected[:, 2 * D :].astype(jnp.bfloat16).reshape(row_total_count, HEADS, head_dim)
    passage_scores = jnp.einsum(
        "qhd,khd->hqk", queries, keys, preferred_element_type=jnp.float32
    ) * head_dim ** (-0.5)
    passage_scores = jnp.where(same_sequence[None], passage_scores, -1000000000.0)
    log_total = jax.nn.logsumexp(passage_scores, -1, keepdims=True)
    attn_probs = jnp.exp(passage_scores - log_total)
    probs_low = attn_probs.astype(jnp.bfloat16)
    context = jnp.einsum("hqk,khd->qhd", probs_low, values, preferred_element_type=jnp.float32)
    context = context.reshape(row_total_count, D).astype(jnp.bfloat16)
    residual = encoder_part_entry.astype(jnp.float32) + jnp.dot(
        context, weight_in[:, 3 * D :], preferred_element_type=jnp.float32
    )
    return (queries, keys, values, attn_probs, probs_low, context, residual)


def attention_back(
    encoder_part_entry, weight_in, bias_out, norm_gain, norm_shift, same_sequence, grad_out
):
    head_dim = D // HEADS
    row_total_count = encoder_part_entry.shape[0]
    queries, keys, values, attn_probs, probs_low, context, residual = attention_parts(
        encoder_part_entry, weight_in, same_sequence
    )
    residual = residual + bias_out
    unused, norm_pull = jax.vjp(layer_norm, residual, norm_gain, norm_shift)
    grad_residual, grad_gain, grad_shift = norm_pull(grad_out)
    grad_low = grad_residual.astype(jnp.bfloat16)
    grad_wout = jnp.einsum("rc,rd->cd", context, grad_low, preferred_element_type=jnp.float32)
    grad_context = jnp.einsum(
        "rd,cd->rc", grad_low, weight_in[:, 3 * D :], preferred_element_type=jnp.float32
    )
    grad_context = grad_context.astype(jnp.bfloat16).reshape(row_total_count, HEADS, head_dim)
    grad_probs = jnp.einsum(
        "qhd,khd->hqk", grad_context, values, preferred_element_type=jnp.float32
    )
    grad_value = jnp.einsum(
        "hqk,qhd->khd", probs_low, grad_context, preferred_element_type=jnp.float32
    )
    grad_scores = attn_probs * (grad_probs - jnp.sum(attn_probs * grad_probs, -1, keepdims=True))
    grad_scores = grad_scores.astype(jnp.bfloat16)
    grad_query = jnp.einsum(
        "hqk,khd->qhd", grad_scores, keys, preferred_element_type=jnp.float32
    ) * head_dim ** (-0.5)
    grad_key = jnp.einsum(
        "hqk,qhd->khd", grad_scores, queries, preferred_element_type=jnp.float32
    ) * head_dim ** (-0.5)
    grad_project = jnp.concatenate(
        [
            grad_query.reshape(row_total_count, D),
            grad_key.reshape(row_total_count, D),
            grad_value.reshape(row_total_count, D),
        ],
        1,
    ).astype(jnp.bfloat16)
    grad_wqkv = jnp.einsum(
        "rd,rf->df", encoder_part_entry, grad_project, preferred_element_type=jnp.float32
    )
    grad_input = grad_residual + jnp.einsum(
        "rf,df->rd", grad_project, weight_in[:, : 3 * D], preferred_element_type=jnp.float32
    )
    grad_weight = jnp.concatenate([grad_wqkv, grad_wout], 1)
    return (grad_input, grad_weight, jnp.sum(grad_residual, 0), grad_gain, grad_shift)


def feed_forward_parts(encoder_part_entry, weight_in, weight_down, bias_out):
    hidden_pre = jnp.dot(encoder_part_entry, weight_in, preferred_element_type=jnp.float32)
    hidden_act, gelu_pull = jax.vjp(exact_gelu, hidden_pre)
    hidden_low = hidden_act.astype(jnp.bfloat16)
    residual = (
        encoder_part_entry.astype(jnp.float32)
        + jnp.dot(hidden_low, weight_down, preferred_element_type=jnp.float32)
        + bias_out
    )
    return (residual, hidden_low, gelu_pull)


def feed_forward_back(
    encoder_part_entry, weight_in, weight_down, norm_gain, norm_shift, parts, grad_out
):
    residual, hidden_low, gelu_pull = parts
    unused, norm_pull = jax.vjp(layer_norm, residual, norm_gain, norm_shift)
    grad_residual, grad_gain, grad_shift = norm_pull(grad_out)
    grad_low = grad_residual.astype(jnp.bfloat16)
    grad_down = jnp.einsum("rf,rd->fd", hidden_low, grad_low, preferred_element_type=jnp.float32)
    grad_hidden = jnp.einsum("rd,fd->rf", grad_low, weight_down, preferred_element_type=jnp.float32)
    grad_pre = gelu_pull(grad_hidden)[0].astype(jnp.bfloat16)
    grad_weight = jnp.einsum(
        "rd,rf->df", encoder_part_entry, grad_pre, preferred_element_type=jnp.float32
    )
    grad_input = grad_residual + jnp.einsum(
        "rf,df->rd", grad_pre, weight_in, preferred_element_type=jnp.float32
    )
    return (grad_input, grad_weight, grad_down, jnp.sum(grad_residual, 0), grad_gain, grad_shift)


def head_parts(layer_out, projector):
    embed_in = layer_out.astype(jnp.bfloat16)
    projected = jnp.dot(embed_in, projector, preferred_element_type=jnp.float32)
    normed, norm_pull = jax.vjp(normalize, projected)
    embedded = normed.astype(jnp.bfloat16)
    query_row_block = QUERY_COUNT * QUERY_LENGTH
    word_pair_affinity = jnp.einsum(
        "qc,pc->qp",
        embedded[:query_row_block],
        embedded[query_row_block:],
        preferred_element_type=jnp.float32,
    )
    return (embed_in, embedded, norm_pull, word_pair_affinity)


def on_device(
    inputs,
    in_weight,
    down_weight,
    out_bias,
    norm_gains,
    norm_shifts,
    projection,
    passage_lengths,
    positive,
):
    sections = lax.axis_size("section")
    section_index = lax.axis_index("section")
    micro_count = inputs.shape[0]
    row_total_count = inputs.shape[1]
    query_row_block = QUERY_COUNT * QUERY_LENGTH
    queries_all = micro_count * positive.shape[1] * lax.axis_size("batch")
    gathered = lax.all_gather(inputs, "section", axis=2, tiled=True)
    weight_in = in_weight[0].astype(jnp.bfloat16)
    own_down = down_weight.astype(jnp.bfloat16)
    other_down = from_behind(own_down, "section", 1)
    weight_down = jnp.concatenate([other_down, own_down], 0)
    projector = lax.all_gather(projection.astype(jnp.bfloat16), "section", axis=1, tiled=True)
    bias_out = out_bias[0]
    norm_gain = norm_gains[0]
    norm_shift = norm_shifts[0]
    passage_masks, same_masks = jax.vmap(sequence_masks)(passage_lengths[:, 0])
    half_rows = own_down.shape[0]
    empty_rows = jnp.zeros((row_total_count, D), jnp.bfloat16)

    def attention_forward(encoder_part_entry, same_sequence, document_word_validity, chosen):
        residual = attention_parts(encoder_part_entry, weight_in, same_sequence)[6] + bias_out
        return (
            layer_norm(residual, norm_gain, norm_shift).astype(jnp.bfloat16),
            jnp.zeros((), jnp.float32),
        )

    def forward_ffn(encoder_part_entry, same_sequence, document_word_validity, chosen):
        residual = feed_forward_parts(encoder_part_entry, weight_in, weight_down, bias_out)[0]
        return (
            layer_norm(residual, norm_gain, norm_shift).astype(jnp.bfloat16),
            jnp.zeros((), jnp.float32),
        )

    def forward_head(encoder_part_entry, same_sequence, document_word_validity, chosen):
        residual = feed_forward_parts(encoder_part_entry, weight_in, weight_down, bias_out)[0]
        layer_out = layer_norm(residual, norm_gain, norm_shift)
        word_pair_affinity = head_parts(layer_out, projector)[3]
        return (empty_rows, maxsim_loss(word_pair_affinity, document_word_validity, chosen))

    def forward_spare(encoder_part_entry, same_sequence, document_word_validity, chosen):
        return (empty_rows, jnp.zeros((), jnp.float32))

    inference_sweep_order = [
        attention_forward,
        forward_ffn,
        attention_forward,
        forward_head,
        forward_spare,
    ]

    def zero_grads():
        return (
            jnp.zeros((row_total_count, D), jnp.float32),
            jnp.zeros((D, FF), jnp.float32),
            jnp.zeros((FF, D), jnp.float32),
            jnp.zeros((D,), jnp.float32),
            jnp.zeros((D,), jnp.float32),
            jnp.zeros((D,), jnp.float32),
            jnp.zeros((D, projector.shape[1]), jnp.float32),
        )

    def attention_backward(
        encoder_part_entry, grad_out, same_sequence, document_word_validity, chosen
    ):
        blank = zero_grads()
        grad_input, grad_weight, grad_bias, grad_gain, grad_shift = attention_back(
            encoder_part_entry, weight_in, bias_out, norm_gain, norm_shift, same_sequence, grad_out
        )
        return (grad_input, grad_weight, blank[2], grad_bias, grad_gain, grad_shift, blank[6])

    def backward_ffn(encoder_part_entry, grad_out, same_sequence, document_word_validity, chosen):
        blank = zero_grads()
        parts = feed_forward_parts(encoder_part_entry, weight_in, weight_down, bias_out)
        grads = feed_forward_back(
            encoder_part_entry, weight_in, weight_down, norm_gain, norm_shift, parts, grad_out
        )
        return grads + (blank[6],)

    def backward_head(encoder_part_entry, grad_out, same_sequence, document_word_validity, chosen):
        parts = feed_forward_parts(encoder_part_entry, weight_in, weight_down, bias_out)
        layer_out = layer_norm(parts[0], norm_gain, norm_shift)
        embed_in, embedded, norm_pull, word_pair_affinity = head_parts(layer_out, projector)
        unused, loss_pull = jax.vjp(
            partial(maxsim_loss, document_word_validity=document_word_validity, positive=chosen),
            word_pair_affinity,
        )
        grad_sim = loss_pull(jnp.asarray(1.0 / queries_all, jnp.float32))[0].astype(jnp.bfloat16)
        grad_query = jnp.einsum(
            "qp,pc->qc", grad_sim, embedded[query_row_block:], preferred_element_type=jnp.float32
        )
        grad_passage = jnp.einsum(
            "qp,qc->pc", grad_sim, embedded[:query_row_block], preferred_element_type=jnp.float32
        )
        grad_projected = norm_pull(jnp.concatenate([grad_query, grad_passage], 0))[0].astype(
            jnp.bfloat16
        )
        grad_projector = jnp.einsum(
            "rd,rc->dc", embed_in, grad_projected, preferred_element_type=jnp.float32
        )
        grad_layer = jnp.einsum(
            "rc,dc->rd", grad_projected, projector, preferred_element_type=jnp.float32
        )
        grads = feed_forward_back(
            encoder_part_entry, weight_in, weight_down, norm_gain, norm_shift, parts, grad_layer
        )
        return grads + (grad_projector,)

    def backward_spare(encoder_part_entry, grad_out, same_sequence, document_word_validity, chosen):
        return zero_grads()

    backward_steps = [
        attention_backward,
        backward_ffn,
        attention_backward,
        backward_head,
        backward_spare,
    ]

    def forward_tick(step_index, carry):
        held_inputs, arriving, loss_sum = carry
        micro_index = step_index - section_index
        active = (micro_index >= 0) & (micro_index < micro_count)
        micro_slot = jnp.clip(micro_index, 0, micro_count - 1)
        encoder_part_entry = jnp.where(section_index == 0, gathered[micro_slot], arriving)
        held_inputs = held_inputs.at[micro_slot].set(
            jnp.where(active, encoder_part_entry, held_inputs[micro_slot])
        )
        branch_id = jnp.where(active, section_index, sections)
        result, loss_part = lax.switch(
            branch_id,
            inference_sweep_order,
            encoder_part_entry,
            same_masks[micro_slot],
            passage_masks[micro_slot],
            positive[micro_slot],
        )
        arriving = jax.tree.map(
            lambda part, own: part.astype(own.dtype),
            from_behind(shortened(result), "section", 1),
            result,
        )
        return (held_inputs, arriving, loss_sum + loss_part)

    held_inputs, arriving, loss_sum = lax.fori_loop(
        0,
        micro_count + sections - 1,
        forward_tick,
        (
            jnp.zeros((micro_count, row_total_count, D), jnp.bfloat16),
            empty_rows,
            jnp.zeros((), jnp.float32),
        ),
    )

    def backward_tick(step_index, carry):
        arriving, input_grads, totals = carry
        micro_index = step_index - (sections - 1 - section_index)
        active = (micro_index >= 0) & (micro_index < micro_count)
        micro_slot = jnp.clip(micro_index, 0, micro_count - 1)
        branch_id = jnp.where(active, section_index, sections)
        grads = lax.switch(
            branch_id,
            backward_steps,
            held_inputs[micro_slot],
            arriving.astype(jnp.float32),
            same_masks[micro_slot],
            passage_masks[micro_slot],
            positive[micro_slot],
        )
        keep_input = active & (section_index == 0)
        input_grads = input_grads.at[micro_slot].add(jnp.where(keep_input, grads[0], 0.0))
        totals = tuple((total + grad for total, grad in zip(totals, grads[1:])))
        arriving = from_behind(grads[0].astype(jnp.bfloat16), "section", -1)
        return (arriving, input_grads, totals)

    blank = zero_grads()
    arriving, input_grads, totals = lax.fori_loop(
        0,
        micro_count + sections - 1,
        backward_tick,
        (empty_rows, jnp.zeros((micro_count, row_total_count, D), jnp.float32), blank[1:]),
    )
    grad_in, grad_down, grad_bias, grad_gain, grad_shift, grad_projector = totals
    odd_section = section_index % 2 == 1
    summed = lax.psum((grad_in, grad_down, grad_bias, grad_gain, grad_shift), "batch")
    moved_half = from_behind(summed[1][:half_rows].astype(jnp.bfloat16), "section", -1).astype(
        jnp.float32
    )
    down_grad = jnp.where(odd_section, summed[1][half_rows:], moved_half)
    in_grad, bias_grad, gain_grad, shift_grad = (summed[0], summed[2], summed[3], summed[4])
    head_total = lax.psum((grad_projector, loss_sum), ("section", "batch"))
    column_count = projection.shape[1]
    projection_grad = lax.dynamic_slice_in_dim(
        head_total[0], section_index * column_count, column_count, 1
    )
    total_loss = head_total[1] / queries_all
    input_grad = lax.psum_scatter(
        input_grads.astype(jnp.bfloat16), "section", scatter_dimension=2, tiled=True
    ).astype(jnp.float32)
    return (
        total_loss,
        input_grad,
        in_grad[None],
        down_grad,
        bias_grad[None],
        gain_grad[None],
        shift_grad[None],
        projection_grad,
    )


def solution(mesh):
    in_specs = (
        P(None, "batch", "section"),
        P("section", None, None),
        P("section", None),
        P("section", None),
        P("section", None),
        P("section", None),
        P(None, "section"),
        P(None, "batch", None),
        P(None, "batch"),
    )
    out_specs = (
        P(),
        P(None, "batch", "section"),
        P("section", None, None),
        P("section", None),
        P("section", None),
        P("section", None),
        P("section", None),
        P(None, "section"),
    )
    return jax.shard_map(
        on_device, mesh=mesh, in_specs=in_specs, out_specs=out_specs, check_vma=False
    )
```

profile of v0, /device:TPU:0, one launch (start us, length us, event | category | flops | bytes accessed | tf_op | source)
XLA Modules:
  0.0 2235.3 jit_solution(14292342368255580300)
XLA Ops:
  19.5 59.6 %all_gather.7 = bf16[768,128]{0,1:T(8,128)(2,1)S(1)} all-gather(bf16[768,32]{0,1:T(8,128)(2,1)S(1)} %convert_element_type.258), channel_id=1, replica_groups=mesh['section'=4,'batch'=8] {'section'}, dimensions={1}, use_global_device_ids=true | all-gather | bytes 245760 | tf_op jit(solution)/shard_map/all_gather | solution.py:224
  105.9 485.4 %while.50 = (s32[]{:T(128)}, bf16[2,768,768]{2,1,0:T(8,128)(2,1)}, bf16[768,768]{1,0:T(8,128)(2,1)S(1)}, f32[]{:T(128)}, s32[]{:T(128)}, /*index=5*/pred[]{:T(51...) while((s32[]{:T(128)}, bf16[2,768,768]{2,1,0:T(8,128)(2,1)}, ...), condition=%wide.region_29.30_spmd.clone, body=%wide.region_2.29_spmd.clone.sunk | while | flops 7583638528 | bytes 151431344 | solution.py:356
  113.0 78.8 %conditional.6 = (bf16[768,768]{1,0:T(8,128)(2,1)}, f32[]{:T(128)}) conditional(s32[]{:T(128)} %clamp.20, (bf16[768,768]{1,0:T(8,128)(2,1)S(1)}, bf16[768,3072]{1,0:T(8,128)(2,1)}, s32[2,768]{1,0:T(2,128)S(1)}, s32[]{:T(128)}, f32[1,768]{1,0:T(1,128)S(1)}, /*index=5*/f32[1,768]{1,0:T(1,128)S(1)}, f32[1,768]{1,0:T(1,128)}, ...), branch_computations={%region_4.8_spmd, %region_9.11_spmd, %region_12.16_spmd, %region_1... | conditional | flops 7581869056 | bytes 138437744 | solution.py:341
  122.5 11.7 fusion.8
  134.2 12.8 exponential_reduce_fusion
  148.2 13.6 fusion.12
  193.2 25.7 %collective-permute-done = bf16[768,768]{1,0:T(8,128)(2,1)S(1)} collective-permute-done((bf16[768,768]{1,0:T(8,128)(2,1)}, bf16[768,768]{1,0:T(8,128)(2,1)S(1)}, u32[]{:S(2)}, u32[]{:S(2)}) %collective-permute-start) | collective-permute-done | bytes 1179680 | tf_op jit(solution)/shard_map/while/body/eval_jaxpr/ppermute | solution.py:24
  226.0 78.8 %conditional.6 = (bf16[768,768]{1,0:T(8,128)(2,1)}, f32[]{:T(128)}) conditional(s32[]{:T(128)} %clamp.20, (bf16[768,768]{1,0:T(8,128)(2,1)S(1)}, bf16[768,3072]{1,0:T(8,128)(2,1)}, s32[2,768]{1,0:T(2,128)S(1)}, s32[]{:T(128)}, f32[1,768]{1,0:T(1,128)S(1)}, /*index=5*/f32[1,768]{1,0:T(1,128)S(1)}, f32[1,768]{1,0:T(1,128)}, ...), branch_computations={%region_4.8_spmd, %region_9.11_spmd, %region_12.16_spmd, %region_1... | conditional | flops 7581869056 | bytes 138437744 | solution.py:341
  235.4 11.7 fusion.8
  247.1 12.8 exponential_reduce_fusion
  261.2 13.6 fusion.12
  306.2 25.2 %collective-permute-done = bf16[768,768]{1,0:T(8,128)(2,1)S(1)} collective-permute-done((bf16[768,768]{1,0:T(8,128)(2,1)}, bf16[768,768]{1,0:T(8,128)(2,1)S(1)}, u32[]{:S(2)}, u32[]{:S(2)}) %collective-permute-start) | collective-permute-done | bytes 1179680 | tf_op jit(solution)/shard_map/while/body/eval_jaxpr/ppermute | solution.py:24
  338.4 25.2 %conditional.6 = (bf16[768,768]{1,0:T(8,128)(2,1)}, f32[]{:T(128)}) conditional(s32[]{:T(128)} %clamp.20, (bf16[768,768]{1,0:T(8,128)(2,1)S(1)}, bf16[768,3072]{1,0:T(8,128)(2,1)}, s32[2,768]{1,0:T(2,128)S(1)}, s32[]{:T(128)}, f32[1,768]{1,0:T(1,128)S(1)}, /*index=5*/f32[1,768]{1,0:T(1,128)S(1)}, f32[1,768]{1,0:T(1,128)}, ...), branch_computations={%region_4.8_spmd, %region_9.11_spmd, %region_12.16_spmd, %region_1... | conditional | flops 7581869056 | bytes 138437744 | solution.py:341
  363.6 37.4 %collective-permute-start = (bf16[768,768]{1,0:T(8,128)(2,1)}, bf16[768,768]{1,0:T(8,128)(2,1)S(1)}, u32[]{:S(2)}, u32[]{:S(2)}) collective-permute-start(bf16[768,768]{1,0:T(8,128)(2,1)} %get-tuple-element.2007), channel_id=1, source_target_pairs={{0,8},{8,16},{16,24},{1,9},{9,17},{17,25},{2,10},{10,18},{18,26},{... | collective-permute-start | bytes 3538952 | tf_op jit(solution)/shard_map/while/body/eval_jaxpr/ppermute | solution.py:24
  401.0 24.2 %collective-permute-done = bf16[768,768]{1,0:T(8,128)(2,1)S(1)} collective-permute-done((bf16[768,768]{1,0:T(8,128)(2,1)}, bf16[768,768]{1,0:T(8,128)(2,1)S(1)}, u32[]{:S(2)}, u32[]{:S(2)}) %collective-permute-start) | collective-permute-done | bytes 1179680 | tf_op jit(solution)/shard_map/while/body/eval_jaxpr/ppermute | solution.py:24
  432.3 25.2 %conditional.6 = (bf16[768,768]{1,0:T(8,128)(2,1)}, f32[]{:T(128)}) conditional(s32[]{:T(128)} %clamp.20, (bf16[768,768]{1,0:T(8,128)(2,1)S(1)}, bf16[768,3072]{1,0:T(8,128)(2,1)}, s32[2,768]{1,0:T(2,128)S(1)}, s32[]{:T(128)}, f32[1,768]{1,0:T(1,128)S(1)}, /*index=5*/f32[1,768]{1,0:T(1,128)S(1)}, f32[1,768]{1,0:T(1,128)}, ...), branch_computations={%region_4.8_spmd, %region_9.11_spmd, %region_12.16_spmd, %region_1... | conditional | flops 7581869056 | bytes 138437744 | solution.py:341
  461.9 23.3 %collective-permute-done = bf16[768,768]{1,0:T(8,128)(2,1)S(1)} collective-permute-done((bf16[768,768]{1,0:T(8,128)(2,1)}, bf16[768,768]{1,0:T(8,128)(2,1)S(1)}, u32[]{:S(2)}, u32[]{:S(2)}) %collective-permute-start) | collective-permute-done | bytes 1179680 | tf_op jit(solution)/shard_map/while/body/eval_jaxpr/ppermute | solution.py:24
  492.3 25.2 %conditional.6 = (bf16[768,768]{1,0:T(8,128)(2,1)}, f32[]{:T(128)}) conditional(s32[]{:T(128)} %clamp.20, (bf16[768,768]{1,0:T(8,128)(2,1)S(1)}, bf16[768,3072]{1,0:T(8,128)(2,1)}, s32[2,768]{1,0:T(2,128)S(1)}, s32[]{:T(128)}, f32[1,768]{1,0:T(1,128)S(1)}, /*index=5*/f32[1,768]{1,0:T(1,128)S(1)}, f32[1,768]{1,0:T(1,128)}, ...), branch_computations={%region_4.8_spmd, %region_9.11_spmd, %region_12.16_spmd, %region_1... | conditional | flops 7581869056 | bytes 138437744 | solution.py:341
  517.5 49.8 %collective-permute-start = (bf16[768,768]{1,0:T(8,128)(2,1)}, bf16[768,768]{1,0:T(8,128)(2,1)S(1)}, u32[]{:S(2)}, u32[]{:S(2)}) collective-permute-start(bf16[768,768]{1,0:T(8,128)(2,1)} %get-tuple-element.2007), channel_id=1, source_target_pairs={{0,8},{8,16},{16,24},{1,9},{9,17},{17,25},{2,10},{10,18},{18,26},{... | collective-permute-start | bytes 3538952 | tf_op jit(solution)/shard_map/while/body/eval_jaxpr/ppermute | solution.py:24
  567.4 22.7 %collective-permute-done = bf16[768,768]{1,0:T(8,128)(2,1)S(1)} collective-permute-done((bf16[768,768]{1,0:T(8,128)(2,1)}, bf16[768,768]{1,0:T(8,128)(2,1)S(1)}, u32[]{:S(2)}, u32[]{:S(2)}) %collective-permute-start) | collective-permute-done | bytes 1179680 | tf_op jit(solution)/shard_map/while/body/eval_jaxpr/ppermute | solution.py:24
  593.9 1026.4 %while.51 = (s32[]{:T(128)}, bf16[768,768]{0,1:T(8,128)(2,1)S(1)}, f32[2,768,768]{1,2,0:T(8,128)}, f32[768,3072]{0,1:T(8,128)}, f32[3072,768]{1,0:T(8,128)}, /*i...) while((s32[]{:T(128)}, bf16[768,768]{0,1:T(8,128)(2,1)S(1)}, ...), condition=%wide.region_80.81_spmd.clone, body=%wide.region_31.80_spmd.clone.sunk | while | flops 22482866176 | bytes 566789248 | solution.py:389
  598.3 44.7 %conditional.7 = (f32[768,768]{0,1:T(8,128)S(1)}, f32[768,3072]{0,1:T(8,128)}, f32[3072,768]{1,0:T(8,128)}, f32[768]{0:T(1024)}, f32[768]{0:T(1024)}, /*index=5*/f32[768]{0:T(1024)}, f32[768,128]{1,0:T(8,128)}) conditional(s32[]{:T(128)} %clamp.21, (f32[1,768]{1,0:T(1,128)S(1)}, f32[768,768]{0,1:T(8,128)S(1)}, ...), branch_computations={%region_32.42_spmd, %region_43.50_spmd, %region_51.61_spmd, %regio... | conditional | flops 22470279168 | bytes 466400672 | solution.py:373
  646.8 8.8 select_add_fusion.11
  665.3 8.5 select_add_fusion.12
  677.7 44.6 %conditional.7 = (f32[768,768]{0,1:T(8,128)S(1)}, f32[768,3072]{0,1:T(8,128)}, f32[3072,768]{1,0:T(8,128)}, f32[768]{0:T(1024)}, f32[768]{0:T(1024)}, /*index=5*/f32[768]{0:T(1024)}, f32[768,128]{1,0:T(8,128)}) conditional(s32[]{:T(128)} %clamp.21, (f32[1,768]{1,0:T(1,128)S(1)}, f32[768,768]{0,1:T(8,128)S(1)}, ...), branch_computations={%region_32.42_spmd, %region_43.50_spmd, %region_51.61_spmd, %regio... | conditional | flops 22470279168 | bytes 466400672 | solution.py:373
  726.1 11.5 select_add_fusion.11
  747.4 11.1 select_add_fusion.12
  758.5 23.9 %collective-permute-done.1 = bf16[768,768]{0,1:T(8,128)(2,1)S(1)} collective-permute-done((bf16[768,768]{0,1:T(8,128)(2,1)}, bf16[768,768]{0,1:T(8,128)(2,1)S(1)}, u32[]{:S(2)}, u32[]{:S(2)}) %collective-permute-start.1) | collective-permute-done | bytes 1179680 | tf_op jit(solution)/shard_map/while/body/eval_jaxpr/ppermute | solution.py:24
  786.6 44.4 %conditional.7 = (f32[768,768]{0,1:T(8,128)S(1)}, f32[768,3072]{0,1:T(8,128)}, f32[3072,768]{1,0:T(8,128)}, f32[768]{0:T(1024)}, f32[768]{0:T(1024)}, /*index=5*/f32[768]{0:T(1024)}, f32[768,128]{1,0:T(8,128)}) conditional(s32[]{:T(128)} %clamp.21, (f32[1,768]{1,0:T(1,128)S(1)}, f32[768,768]{0,1:T(8,128)S(1)}, ...), branch_computations={%region_32.42_spmd, %region_43.50_spmd, %region_51.61_spmd, %regio... | conditional | flops 22470279168 | bytes 466400672 | solution.py:373
  834.9 11.5 select_add_fusion.11
  856.2 11.1 select_add_fusion.12
  867.3 279.3 %collective-permute-done.1 = bf16[768,768]{0,1:T(8,128)(2,1)S(1)} collective-permute-done((bf16[768,768]{0,1:T(8,128)(2,1)}, bf16[768,768]{0,1:T(8,128)(2,1)S(1)}, u32[]{:S(2)}, u32[]{:S(2)}) %collective-permute-start.1) | collective-permute-done | bytes 1179680 | tf_op jit(solution)/shard_map/while/body/eval_jaxpr/ppermute | solution.py:24
  1150.7 195.2 %conditional.7 = (f32[768,768]{0,1:T(8,128)S(1)}, f32[768,3072]{0,1:T(8,128)}, f32[3072,768]{1,0:T(8,128)}, f32[768]{0:T(1024)}, f32[768]{0:T(1024)}, /*index=5*/f32[768]{0:T(1024)}, f32[768,128]{1,0:T(8,128)}) conditional(s32[]{:T(128)} %clamp.21, (f32[1,768]{1,0:T(1,128)S(1)}, f32[768,768]{0,1:T(8,128)S(1)}, ...), branch_computations={%region_32.42_spmd, %region_43.50_spmd, %region_51.61_spmd, %regio... | conditional | flops 22470279168 | bytes 466400672 | solution.py:373
  1162.1 13.1 fusion.123
  1175.2 12.7 exponential_reduce_fusion.3
  1190.3 13.8 convolution_convert_fusion.5
  1216.3 23.6 %multiply_reduce_fusion.6 = (f32[12,768]{1,0:T(8,128)S(1)}, f32[12,768,768]{1,2,0:T(8,128)}) fusion(f32[12,768,768]{1,2,0:T(8,128)} %get-tuple-element.1741, f32[12,768]{1,0:T(8,128)S(1)} %log_add_fusion.2, pred[768,768]{0,1:T(8,128)(4,1)S(1)} %compare_bitcast_fusion.2, bf16[768,12,64]{0,2,1:T(8,128)(2,1)S(1)} %bitcast.197, ...), kind=kOutput, calls=%fused_computation.195 | convolution fusion | flops 941349888 | bytes 59645952 | tf_op jit(solution)/shard_map/while/body/eval_jaxpr/cond/branch_0_fun/qhd,khd->hqk/dot_general | solution.py:124
  1239.9 23.6 %multiply_convert_fusion.1 = bf16[12,768,768]{1,2,0:T(8,128)(2,1)} fusion(f32[12,768,768]{1,2,0:T(8,128)} %get-tuple-element.1745, f32[12,768,768]{1,2,0:T(8,128)} %get-tuple-element.1741, f32[12,768]{1,0:T(8,128)S(1)} %get-tuple-element.1744, f32[12,768]{1,0:T(8,128)S(1)} %log_add_fusion.2, pred[768,768]{0,1:T(8,128)(4,1)S(1)} %compare_bitcast_fusion.2), kind=kLoop, calls=%fused_computation.194 | loop fusion | flops 42467328 | bytes 71442432 | tf_op jit(solution)/shard_map/while/body/eval_jaxpr/cond/branch_0_fun/convert_element_type | solution.py:131
  1263.5 8.7 multiply_convert_fusion.3
  1272.2 10.6 multiply_convert_fusion.2
  1282.8 14.4 convolution_convert_fusion.4
  1297.2 7.9 convolution_bitcast_fusion
  1306.3 7.2 pad_maximum_fusion
  1349.7 11.5 select_add_fusion.11
  1371.0 11.1 select_add_fusion.12
  1386.0 195.2 %conditional.7 = (f32[768,768]{0,1:T(8,128)S(1)}, f32[768,3072]{0,1:T(8,128)}, f32[3072,768]{1,0:T(8,128)}, f32[768]{0:T(1024)}, f32[768]{0:T(1024)}, /*index=5*/f32[768]{0:T(1024)}, f32[768,128]{1,0:T(8,128)}) conditional(s32[]{:T(128)} %clamp.21, (f32[1,768]{1,0:T(1,128)S(1)}, f32[768,768]{0,1:T(8,128)S(1)}, ...), branch_computations={%region_32.42_spmd, %region_43.50_spmd, %region_51.61_spmd, %regio... | conditional | flops 22470279168 | bytes 466400672 | solution.py:373
  1397.5 13.1 fusion.123
  1410.5 12.7 exponential_reduce_fusion.3
  1425.6 13.8 convolution_convert_fusion.5
  1451.7 23.7 %multiply_reduce_fusion.6 = (f32[12,768]{1,0:T(8,128)S(1)}, f32[12,768,768]{1,2,0:T(8,128)}) fusion(f32[12,768,768]{1,2,0:T(8,128)} %get-tuple-element.1741, f32[12,768]{1,0:T(8,128)S(1)} %log_add_fusion.2, pred[768,768]{0,1:T(8,128)(4,1)S(1)} %compare_bitcast_fusion.2, bf16[768,12,64]{0,2,1:T(8,128)(2,1)S(1)} %bitcast.197, ...), kind=kOutput, calls=%fused_computation.195 | convolution fusion | flops 941349888 | bytes 59645952 | tf_op jit(solution)/shard_map/while/body/eval_jaxpr/cond/branch_0_fun/qhd,khd->hqk/dot_general | solution.py:124
  1475.4 23.6 %multiply_convert_fusion.1 = bf16[12,768,768]{1,2,0:T(8,128)(2,1)} fusion(f32[12,768,768]{1,2,0:T(8,128)} %get-tuple-element.1745, f32[12,768,768]{1,2,0:T(8,128)} %get-tuple-element.1741, f32[12,768]{1,0:T(8,128)S(1)} %get-tuple-element.1744, f32[12,768]{1,0:T(8,128)S(1)} %log_add_fusion.2, pred[768,768]{0,1:T(8,128)(4,1)S(1)} %compare_bitcast_fusion.2), kind=kLoop, calls=%fused_computation.194 | loop fusion | flops 42467328 | bytes 71442432 | tf_op jit(solution)/shard_map/while/body/eval_jaxpr/cond/branch_0_fun/convert_element_type | solution.py:131
  1499.0 8.7 multiply_convert_fusion.3
  1507.7 10.6 multiply_convert_fusion.2
  1518.2 14.2 convolution_convert_fusion.4
  1532.4 7.9 convolution_bitcast_fusion
  1541.5 7.2 pad_maximum_fusion
  1585.0 11.5 select_add_fusion.11
  1606.3 11.1 select_add_fusion.12
  1620.3 9.7 copy.203
  1636.0 368.6 %all-reduce.7.cloned.1.call-done = (f32[1,768,3072]{2,1,0:T(8,128)}, f32[3072,768]{1,0:T(8,128)}) async-done(((f32[1,768,3072]{2,1,0:T(8,128)}, f32[3072,768]{1,0:T(8,128)}), (f32[1,768,3072]{2,1,0:T(8,128)}, f32[3072,768]{1,0:T(8,128)})) %all-reduce.7.cloned.1.call-update) | async-done | bytes 18874384 | tf_op jit(solution)/shard_map/psum | solution.py:397
  2008.5 87.8 %psum.49 = f32[]{:T(128)} all-reduce(f32[]{:T(128)} %get-tuple-element.1126), channel_id=1, replica_groups=mesh['section'=4,'batch'=8] {'section','batch'}, use_global_device_ids=true, to_apply=%region_30.31 | all-reduce | flops 1 | bytes 8 | tf_op jit(solution)/shard_map/psum | solution.py:403
  2097.0 15.2 all-reduce
  2112.3 61.5 %all-reduce.5.cloned.1.call-done = f32[768,128]{0,1:T(8,128)} async-done(((f32[768,128]{0,1:T(8,128)}), f32[768,128]{0,1:T(8,128)}) %all-reduce.5.cloned.1.call-update) | async-done | bytes 393232 | tf_op jit(solution)/shard_map/psum | solution.py:403
  2175.3 38.7 %reduce-scatter.2.cloned.1.call-done = bf16[2,768,192]{1,2,0:T(8,128)(2,1)} async-done(((bf16[2,768,768]{1,2,0:T(8,128)(2,1)}), bf16[2,768,192]{1,2,0:T(8,128)(2,1)}) %reduce-scatter.2.cloned.1.call-update) | async-done | bytes 589840 | tf_op jit(solution)/shard_map/reduce_scatter | solution.py:409
  (397 shorter events, 348.8 us)
Async XLA Ops:
  7.2 11.4 copy-start.76
  7.2 12.3 copy-start.72
  7.2 90.2 %all-gather.2.cloned.1.call-start = ((), (), s32[]{:S(2)}) async-start(), calls=%async_computation.1 | async-start | bytes 2949120 | tf_op jit(solution)/shard_map/all_gather | solution.py:219
  9.7 1994.9 %all-reduce.7.cloned.1.call-start = ((), (), s32[]{:S(2)}) async-start(), calls=%async_computation.4 | async-start | bytes 37748736 | tf_op jit(solution)/shard_map/psum | solution.py:397
  12.4 74.6 %collective-permute-start.2 = (bf16[1536,768]{1,0:T(8,128)(2,1)S(1)}, bf16[1536,768]{1,0:T(8,128)(2,1)}, u32[]{:S(2)}, u32[]{:S(2)}) collective-permute-start(bf16[1536,768]{1,0:T(8,128)(2,1)S(1)} %convert_element_type.257), channel_id=1, source_target_pairs={{0,8},{8,16},{16,24},{1,9},{9,17},{17,25},{2,10},{10,18},{18,26},{... | collective-permute-start | bytes 7077896 | tf_op jit(solution)/shard_map/ppermute | solution.py:24
  91.2 14.7 copy-start.39
  91.2 14.7 copy-start.40
  122.5 11.7 copy-start.19
  134.1 13.4 copy-start.22
  191.8 27.1 %collective-permute-start = (bf16[768,768]{1,0:T(8,128)(2,1)}, bf16[768,768]{1,0:T(8,128)(2,1)S(1)}, u32[]{:S(2)}, u32[]{:S(2)}) collective-permute-start(bf16[768,768]{1,0:T(8,128)(2,1)} %get-tuple-element.2007), channel_id=1, source_target_pairs={{0,8},{8,16},{16,24},{1,9},{9,17},{17,25},{2,10},{10,18},{18,26},{... | collective-permute-start | bytes 3538952 | tf_op jit(solution)/shard_map/while/body/eval_jaxpr/ppermute | solution.py:24
  235.4 11.7 copy-start.19
  247.1 13.4 copy-start.22
  304.8 26.5 %collective-permute-start = (bf16[768,768]{1,0:T(8,128)(2,1)}, bf16[768,768]{1,0:T(8,128)(2,1)S(1)}, u32[]{:S(2)}, u32[]{:S(2)}) collective-permute-start(bf16[768,768]{1,0:T(8,128)(2,1)} %get-tuple-element.2007), channel_id=1, source_target_pairs={{0,8},{8,16},{16,24},{1,9},{9,17},{17,25},{2,10},{10,18},{18,26},{... | collective-permute-start | bytes 3538952 | tf_op jit(solution)/shard_map/while/body/eval_jaxpr/ppermute | solution.py:24
  363.6 61.7 %collective-permute-start = (bf16[768,768]{1,0:T(8,128)(2,1)}, bf16[768,768]{1,0:T(8,128)(2,1)S(1)}, u32[]{:S(2)}, u32[]{:S(2)}) collective-permute-start(bf16[768,768]{1,0:T(8,128)(2,1)} %get-tuple-element.2007), channel_id=1, source_target_pairs={{0,8},{8,16},{16,24},{1,9},{9,17},{17,25},{2,10},{10,18},{18,26},{... | collective-permute-start | bytes 3538952 | tf_op jit(solution)/shard_map/while/body/eval_jaxpr/ppermute | solution.py:24
  457.5 27.7 %collective-permute-start = (bf16[768,768]{1,0:T(8,128)(2,1)}, bf16[768,768]{1,0:T(8,128)(2,1)S(1)}, u32[]{:S(2)}, u32[]{:S(2)}) collective-permute-start(bf16[768,768]{1,0:T(8,128)(2,1)} %get-tuple-element.2007), channel_id=1, source_target_pairs={{0,8},{8,16},{16,24},{1,9},{9,17},{17,25},{2,10},{10,18},{18,26},{... | collective-permute-start | bytes 3538952 | tf_op jit(solution)/shard_map/while/body/eval_jaxpr/ppermute | solution.py:24
  517.5 72.5 %collective-permute-start = (bf16[768,768]{1,0:T(8,128)(2,1)}, bf16[768,768]{1,0:T(8,128)(2,1)S(1)}, u32[]{:S(2)}, u32[]{:S(2)}) collective-permute-start(bf16[768,768]{1,0:T(8,128)(2,1)} %get-tuple-element.2007), channel_id=1, source_target_pairs={{0,8},{8,16},{16,24},{1,9},{9,17},{17,25},{2,10},{10,18},{18,26},{... | collective-permute-start | bytes 3538952 | tf_op jit(solution)/shard_map/while/body/eval_jaxpr/ppermute | solution.py:24
  645.5 28.3 %collective-permute-start.1 = (bf16[768,768]{0,1:T(8,128)(2,1)}, bf16[768,768]{0,1:T(8,128)(2,1)S(1)}, u32[]{:S(2)}, u32[]{:S(2)}) collective-permute-start(bf16[768,768]{0,1:T(8,128)(2,1)} %convert_element_type.348), channel_id=1, source_target_pairs={{8,0},{16,8},{24,16},{9,1},{17,9},{25,17},{10,2},{18,10},{26,18},{... | collective-permute-start | bytes 3538952 | tf_op jit(solution)/shard_map/while/body/eval_jaxpr/ppermute | solution.py:24
  646.8 13.2 copy-start.18
  655.6 8.5 copy-start.61
  655.6 8.5 copy-start.62
  655.6 8.5 copy-start.66
  655.6 8.5 copy-start.69
  724.8 57.7 %collective-permute-start.1 = (bf16[768,768]{0,1:T(8,128)(2,1)}, bf16[768,768]{0,1:T(8,128)(2,1)S(1)}, u32[]{:S(2)}, u32[]{:S(2)}) collective-permute-start(bf16[768,768]{0,1:T(8,128)(2,1)} %convert_element_type.348), channel_id=1, source_target_pairs={{8,0},{16,8},{24,16},{9,1},{17,9},{25,17},{10,2},{18,10},{26,18},{... | collective-permute-start | bytes 3538952 | tf_op jit(solution)/shard_map/while/body/eval_jaxpr/ppermute | solution.py:24
  726.1 16.0 copy-start.18
  737.6 8.6 copy-start.61
  737.6 8.6 copy-start.62
  737.6 8.6 copy-start.66
  737.6 8.6 copy-start.69
  833.6 313.0 %collective-permute-start.1 = (bf16[768,768]{0,1:T(8,128)(2,1)}, bf16[768,768]{0,1:T(8,128)(2,1)S(1)}, u32[]{:S(2)}, u32[]{:S(2)}) collective-permute-start(bf16[768,768]{0,1:T(8,128)(2,1)} %convert_element_type.348), channel_id=1, source_target_pairs={{8,0},{16,8},{24,16},{9,1},{17,9},{25,17},{10,2},{18,10},{26,18},{... | collective-permute-start | bytes 3538952 | tf_op jit(solution)/shard_map/while/body/eval_jaxpr/ppermute | solution.py:24
  834.9 16.0 copy-start.18
  846.4 8.6 copy-start.61
  846.4 8.6 copy-start.62
  846.4 8.6 copy-start.66
  846.4 8.6 copy-start.69
  1213.0 26.8 %copy-start.13 = (f32[768,768]{0,1:T(8,128)}, f32[768,768]{0,1:T(8,128)S(1)}, u32[]{:S(2)}) copy-start(f32[768,768]{0,1:T(8,128)S(1)} %get-tuple-element.1700) | copy-start | bytes 7077892 | tf_op jit(solution)/shard_map/while/body/eval_jaxpr/cond
  1216.3 23.6 %copy-start.24 = (bf16[768,768]{0,1:T(8,128)(2,1)}, bf16[768,768]{0,1:T(8,128)(2,1)S(1)}, u32[]{:S(2)}) copy-start(bf16[768,768]{0,1:T(8,128)(2,1)S(1)} %convolution_convert_fusion.3) | copy-start | bytes 3538948 | tf_op jit(solution)/shard_map/while/body/eval_jaxpr/cond
  1239.9 23.6 %copy-start.7 = (bf16[768,768]{0,1:T(8,128)(2,1)S(1)}, bf16[768,768]{0,1:T(8,128)(2,1)}, u32[]{:S(2)}) copy-start(bf16[768,768]{0,1:T(8,128)(2,1)} %copy.170) | copy-start | bytes 3538948 | tf_op jit(solution)/shard_map/while/body/eval_jaxpr/cond
  1263.5 8.7 copy-start.9
  1272.2 10.6 copy-start.25
  1282.8 14.4 copy-start.29
  1348.4 33.7 %collective-permute-start.1 = (bf16[768,768]{0,1:T(8,128)(2,1)}, bf16[768,768]{0,1:T(8,128)(2,1)S(1)}, u32[]{:S(2)}, u32[]{:S(2)}) collective-permute-start(bf16[768,768]{0,1:T(8,128)(2,1)} %convert_element_type.348), channel_id=1, source_target_pairs={{8,0},{16,8},{24,16},{9,1},{17,9},{25,17},{10,2},{18,10},{26,18},{... | collective-permute-start | bytes 3538952 | tf_op jit(solution)/shard_map/while/body/eval_jaxpr/ppermute | solution.py:24
  1349.7 16.0 copy-start.18
  1361.2 8.6 copy-start.61
  1361.2 8.6 copy-start.62
  1361.2 8.6 copy-start.66
  1361.2 8.6 copy-start.69
  1448.4 27.0 %copy-start.13 = (f32[768,768]{0,1:T(8,128)}, f32[768,768]{0,1:T(8,128)S(1)}, u32[]{:S(2)}) copy-start(f32[768,768]{0,1:T(8,128)S(1)} %get-tuple-element.1700) | copy-start | bytes 7077892 | tf_op jit(solution)/shard_map/while/body/eval_jaxpr/cond
  1451.7 23.7 %copy-start.24 = (bf16[768,768]{0,1:T(8,128)(2,1)}, bf16[768,768]{0,1:T(8,128)(2,1)S(1)}, u32[]{:S(2)}) copy-start(bf16[768,768]{0,1:T(8,128)(2,1)S(1)} %convolution_convert_fusion.3) | copy-start | bytes 3538948 | tf_op jit(solution)/shard_map/while/body/eval_jaxpr/cond
  1475.4 23.6 %copy-start.7 = (bf16[768,768]{0,1:T(8,128)(2,1)S(1)}, bf16[768,768]{0,1:T(8,128)(2,1)}, u32[]{:S(2)}) copy-start(bf16[768,768]{0,1:T(8,128)(2,1)} %copy.170) | copy-start | bytes 3538948 | tf_op jit(solution)/shard_map/while/body/eval_jaxpr/cond
  1499.0 8.7 copy-start.9
  1507.7 10.6 copy-start.25
  1518.2 14.2 copy-start.29
  1583.7 33.8 %collective-permute-start.1 = (bf16[768,768]{0,1:T(8,128)(2,1)}, bf16[768,768]{0,1:T(8,128)(2,1)S(1)}, u32[]{:S(2)}, u32[]{:S(2)}) collective-permute-start(bf16[768,768]{0,1:T(8,128)(2,1)} %convert_element_type.348), channel_id=1, source_target_pairs={{8,0},{16,8},{24,16},{9,1},{17,9},{25,17},{10,2},{18,10},{26,18},{... | collective-permute-start | bytes 3538952 | tf_op jit(solution)/shard_map/while/body/eval_jaxpr/ppermute | solution.py:24
  1585.0 16.0 copy-start.18
  1596.5 8.6 copy-start.61
  1596.5 8.6 copy-start.62
  1596.5 8.6 copy-start.66
  1596.5 8.6 copy-start.69
  1630.0 543.7 %all-reduce.5.cloned.1.call-start = ((), (), s32[]{:S(2)}) async-start(), calls=%async_computation.3 | async-start | bytes 786432 | tf_op jit(solution)/shard_map/psum | solution.py:403
  1631.9 582.0 %reduce-scatter.2.cloned.1.call-start = ((), (), s32[]{:S(2)}) async-start(), calls=%async_computation.2 | async-start | bytes 2949120 | tf_op jit(solution)/shard_map/reduce_scatter | solution.py:409
  1636.0 460.4 %copy-start.65 = (f32[768]{0:T(1024)S(1)}, f32[768]{0:T(1024)}, u32[]{:S(2)}) copy-start(f32[768]{0:T(1024)} %get-tuple-element.1131) | copy-start | bytes 9220
  1636.0 460.4 %copy-start.68 = (f32[768]{0:T(1024)S(1)}, f32[768]{0:T(1024)}, u32[]{:S(2)}) copy-start(f32[768]{0:T(1024)} %get-tuple-element.1132) | copy-start | bytes 9220
  1636.0 460.4 %copy-start.71 = (f32[768]{0:T(1024)S(1)}, f32[768]{0:T(1024)}, u32[]{:S(2)}) copy-start(f32[768]{0:T(1024)} %get-tuple-element.1133) | copy-start | bytes 9220
  2007.2 208.9 %collective-permute-start.3 = (bf16[1536,768]{1,0:T(8,128)(2,1)S(1)}, bf16[1536,768]{1,0:T(8,128)(2,1)}, u32[]{:S(2)}, u32[]{:S(2)}) collective-permute-start(bf16[1536,768]{1,0:T(8,128)(2,1)S(1)} %slice.257), channel_id=1, source_target_pairs={{8,0},{16,8},{24,16},{9,1},{17,9},{25,17},{10,2},{18,10},{26,18},{... | collective-permute-start | bytes 7077896 | tf_op jit(solution)/shard_map/ppermute | solution.py:24
  (30 other events, 72.7 us)
Sparse Core Ops, SparseCore 0:
  10.4 86.9 all-gather.1
  1630.2 374.3 all-reduce.6
  2010.5 163.1 all-reduce.4
  2177.5 36.4 reduce-scatter.1
where the time goes:
time: 2240 us
  waiting for transfers between devices  899 us (40%)
  other arithmetic  343 us (15%)
  matrix products  288 us (13%)
  loops' own time  263 us (12%)
  blocking collectives  163 us (7%)
  local copies, waits for them, and re-layouts  155 us (7%)
  starting transfers between devices  108 us (5%)
    ppermute x12, waiting for transfers between devices, from_behind(): return lax.ppermute(block, axis, route)  424 us
    psum x1, waiting for transfers between devices, on_device(): lax.psum((grad_in, grad_down, grad_bias, grad_gain, grad_shift), 'batch')  369 us
    another operation x5, loops' own time, backward_tick(): lax.switch(branch_id, backward_steps, held_inputs[micro_slot], arriving.a...  141 us
    add x25, other arithmetic, backward_tick(): totals = tuple((total + grad for total, grad in zip(totals, grads[1:])))  124 us
    another operation x5, loops' own time, forward_tick(): lax.switch(branch_id, inference_sweep_order, encoder_part_entry, same_mas...  114 us
    ppermute x12, starting transfers between devices, from_behind(): return lax.ppermute(block, axis, route)  108 us
    psum x1, blocking collectives, on_device(): head_total = lax.psum((grad_projector, loss_sum), ('section', 'batch'))  87.8 us
    psum x1, waiting for transfers between devices, on_device(): head_total = lax.psum((grad_projector, loss_sum), ('section', 'batch'))  61.5 us
  transfers between devices with their start and end apart: 16, of which 11 were waited for; matrix products, arithmetic and copies ran while one was open for 8% of the time, Pallas kernels for 0%

commit v1 on v0

v1 whole, which is shorter than its diff:
```python
from functools import partial

import jax
import jax.numpy as jnp
from jax import lax
from jax.experimental import pallas as pl
from jax.experimental.pallas import tpu as pltpu
from jax.sharding import PartitionSpec as P

D = 768
HEADS = 12
FF = 3072
DIM = 128
QUERY_LENGTH = 32
QUERY_COUNT = 4
PASSAGE_COUNT = 3
PASSAGE_TOKENS = 640
PLEN = 512
QROWS = QUERY_LENGTH * QUERY_COUNT
ROWS = QROWS + PASSAGE_TOKENS
REST = PASSAGE_TOKENS - PLEN
SOFTMAX_DIVISOR = 0.1
SIMILARITY_SCALE = 0.25
NORM_EPSILON = 1e-06
MASKED = -1000000000.0
BF = jnp.bfloat16
F32 = jnp.float32
BLOCKS = ((0, QROWS), (QROWS, PLEN), (QROWS + PLEN, REST))
PAIRS = HEADS // 4
HALF = D // 2


def mm(a, b, dims=((1,), (0,))):
    return lax.dot_general(a, b, (dims, ((), ())), preferred_element_type=F32)


def block_mask(which, bound, rows):
    t = lax.broadcasted_iota(jnp.int32, (rows, rows), 0)
    r = lax.broadcasted_iota(jnp.int32, (rows, rows), 1)
    if which == 0:
        return (t // QUERY_LENGTH) == (r // QUERY_LENGTH)
    return (t < bound) == (r < bound)


def attention_kernel(bound_ref, qkv_ref, ctx_ref, lse_ref):
    lane = lax.broadcasted_iota(jnp.int32, (1, 128), 1)
    for which, (start, size) in enumerate(BLOCKS):
        chunk = min(size, 256)
        k = qkv_ref[start : start + size, 128:256]
        v = qkv_ref[start : start + size, 256:384]
        for at in range(start, start + size, chunk):
            q = qkv_ref[at : at + chunk, 0:128]
            total = None
            for head in range(2):
                mine = (lane < 64) if head == 0 else (lane >= 64)
                qm = jnp.where(mine, q, jnp.zeros_like(q)) * BF(0.125)
                vm = jnp.where(mine, v, jnp.zeros_like(v))
                s = mm(k, qm, ((1,), (1,)))
                if which != 1:
                    s = jnp.where(block_mask(which, bound_ref[0], size), s, MASKED)
                top = jnp.max(s, axis=0, keepdims=True)
                e = jnp.exp(s - top)
                weight = jnp.sum(e, axis=0, keepdims=True)
                part = mm(vm, e.astype(BF), ((0,), (0,))) * (1.0 / weight)
                total = part if total is None else total + part
                lse_ref[0, head : head + 1, at : at + chunk] = top + jnp.log(weight)
            ctx_ref[at : at + chunk, :] = total.T.astype(BF)


def attention(qkv, bound):
    return pl.pallas_call(
        attention_kernel,
        grid=(PAIRS,),
        in_specs=[
            pl.BlockSpec(memory_space=pltpu.SMEM),
            pl.BlockSpec((ROWS, 384), lambda i: (0, i)),
        ],
        out_specs=[
            pl.BlockSpec((ROWS, 128), lambda i: (0, i)),
            pl.BlockSpec((1, 8, ROWS), lambda i: (i, 0, 0)),
        ],
        out_shape=[
            jax.ShapeDtypeStruct((ROWS, HALF), BF),
            jax.ShapeDtypeStruct((PAIRS, 8, ROWS), F32),
        ],
        compiler_params=pltpu.CompilerParams(vmem_limit_bytes=32 * 1024 * 1024),
        cost_estimate=pl.CostEstimate(
            flops=12 * 4 * 512 * 512 * 64, bytes_accessed=3000000, transcendentals=2000000
        ),
    )(bound, qkv)


def attention_back_kernel(bound_ref, qkv_ref, dc_ref, lse_ref, out_ref):
    lane = lax.broadcasted_iota(jnp.int32, (1, 128), 1)
    for which, (start, size) in enumerate(BLOCKS):
        chunk = min(size, 256)
        k = qkv_ref[start : start + size, 128:256]
        v = qkv_ref[start : start + size, 256:384]
        dk = jnp.zeros((size, 128), F32)
        dv = jnp.zeros((size, 128), F32)
        for at in range(start, start + size, chunk):
            q = qkv_ref[at : at + chunk, 0:128]
            dc = dc_ref[at : at + chunk, :]
            dq = None
            for head in range(2):
                mine = (lane < 64) if head == 0 else (lane >= 64)
                qm = jnp.where(mine, q, jnp.zeros_like(q)) * BF(0.125)
                dcm = jnp.where(mine, dc, jnp.zeros_like(dc))
                km = jnp.where(mine, k, jnp.zeros_like(k))
                s = mm(k, qm, ((1,), (1,)))
                if which != 1:
                    s = jnp.where(block_mask(which, bound_ref[0], size), s, MASKED)
                p = jnp.exp(s - lse_ref[0, head : head + 1, at : at + chunk])
                dp = mm(v, dcm, ((1,), (1,)))
                inner = jnp.sum(p * dp, axis=0, keepdims=True)
                ds = (p * (dp - inner)).astype(BF)
                dv = dv + mm(p.astype(BF), dcm)
                dk = dk + mm(ds, qm)
                part = mm(km, ds, ((0,), (0,)))
                dq = part if dq is None else dq + part
            out_ref[at : at + chunk, 0:128] = (dq.T * 0.125).astype(BF)
        out_ref[start : start + size, 128:256] = dk.astype(BF)
        out_ref[start : start + size, 256:384] = dv.astype(BF)


def attention_back(qkv, dc, lse, bound):
    return pl.pallas_call(
        attention_back_kernel,
        grid=(PAIRS,),
        in_specs=[
            pl.BlockSpec(memory_space=pltpu.SMEM),
            pl.BlockSpec((ROWS, 384), lambda i: (0, i)),
            pl.BlockSpec((ROWS, 128), lambda i: (0, i)),
            pl.BlockSpec((1, 8, ROWS), lambda i: (i, 0, 0)),
        ],
        out_specs=pl.BlockSpec((ROWS, 384), lambda i: (0, i)),
        out_shape=jax.ShapeDtypeStruct((ROWS, 3 * HALF), BF),
        compiler_params=pltpu.CompilerParams(vmem_limit_bytes=32 * 1024 * 1024),
        cost_estimate=pl.CostEstimate(
            flops=12 * 10 * 512 * 512 * 64, bytes_accessed=5000000, transcendentals=2000000
        ),
    )(bound, qkv, dc, lse)


MESH = pl.DeviceIdType.MESH
EXTRA = 32
FRONT = 1152


def neighbours():
    s, b = lax.axis_index("section"), lax.axis_index("batch")
    x = s + 1 - 2 * (s % 2)
    y = s + 2 - 4 * (s // 2)
    xy = 3 - s
    return s, b, x, y, xy


def greet(layers):
    s, b, x, y, xy = neighbours()
    z, core = b // 2, b % 2
    barrier = pltpu.get_barrier_semaphore()

    def signal(to):
        pl.semaphore_signal(barrier, inc=1, device_id=to, device_id_type=MESH)

    signal((x, b))
    signal((y, b))
    signal((xy, b))
    signal((s, b + 1 - 2 * core))
    if layers > 1:

        @pl.when(z > 0)
        def _():
            signal((s, b - 2))

        @pl.when(z < layers - 1)
        def _():
            signal((s, b + 2))

        ends = (layers - 1 - z) // (layers - 1) + z // (layers - 1)
        pl.semaphore_wait(barrier, 6 - ends)
    else:
        pl.semaphore_wait(barrier, 4)


def fetch_kernel(
    layers,
    spread,
    w_ref,
    down_ref,
    tail_ref,
    vec_ref,
    slices_ref,
    ints_ref,
    first_all,
    rest_all,
    vec_all,
    parts_all,
    ints_other,
    wide,
    out_stage,
    down_stage,
    first,
    rest,
    load_sem,
    own_sem,
    send_sem,
    recv_sem,
    z_send,
    z_recv,
    in_send,
    in_recv,
):
    s, b, x, y, xy = neighbours()
    z, core = b // 2, b % 2
    micro = s // 2
    mine = core == s % 2
    twin = b + 1 - 2 * core

    def load(src, dst, i):
        return pltpu.make_async_copy(src, dst, load_sem.at[i])

    loads = [load(down_ref.at[pl.ds(core * D, D), :], down_stage, 0)]
    even, odd = [], []
    for i in range(PAIRS):
        for t in range(3):
            at = pl.multiple_of(t * D + core * HALF + i * 128, 128)
            to = (3 * i + t) * 128
            even.append(
                load(w_ref.at[:, pl.ds(at, 128)], wide.at[:, pl.ds(to, 128)], 1 + 3 * i + t)
            )
    even.append(load(w_ref.at[pl.ds(core * HALF, HALF), pl.ds(3 * D, D)], out_stage, 10))
    for i in range(2):
        at = pl.multiple_of(i * 2 * D + core * D, 128)
        odd.append(load(w_ref.at[:, pl.ds(at, D)], wide.at[:, pl.ds(i * D, D)], 11 + i))
    loads[0].start()

    @pl.when(s % 2 == 0)
    def _():
        for copy in even:
            copy.start()

    @pl.when(s % 2 == 1)
    def _():
        for copy in odd:
            copy.start()

    tail = pltpu.make_async_copy(
        tail_ref, rest.at[pl.ds(FRONT, EXTRA), :], load_sem.at[13]
    )
    tail.start()
    greet(layers)

    def feature(i, which, section, to):
        return pltpu.make_async_remote_copy(
            src_ref=slices_ref.at[which],
            dst_ref=parts_all.at[section],
            send_sem=in_send.at[i],
            recv_sem=in_recv.at[i],
            device_id=(to, b),
            device_id_type=MESH,
        )

    def to_twin(i, src, dst):
        return pltpu.make_async_remote_copy(
            src_ref=src,
            dst_ref=dst,
            send_sem=in_send.at[i],
            recv_sem=in_recv.at[i],
            device_id=(s, twin),
            device_id_type=MESH,
        )

    def quarter_to_twin(i, f):
        return to_twin(i, parts_all.at[f], parts_all.at[f])

    swap_ints = to_twin(7, ints_ref, ints_other)
    own_quarter = pltpu.make_async_copy(slices_ref.at[micro], parts_all.at[s], load_sem.at[14])
    swap_ints.start()

    @pl.when(mine)
    def _():
        own_quarter.start()
        feature(1, 1 - micro, s, y).start()

    @pl.when(jnp.logical_not(mine))
    def _():
        feature(0, micro, s, x).start()
        feature(2, 1 - micro, s, xy).start()

    loads[0].wait()

    @pl.loop(0, D // 96)
    def _(i):
        rows = pl.ds(pl.multiple_of(i * 96, 16), 96)
        to = pl.ds(pl.multiple_of(HALF + i * 96, 16), 96)
        rest[to, :] = down_stage[rows, :].astype(BF)

    @pl.when(s % 2 == 0)
    def _():
        for copy in even:
            copy.wait()

        @pl.loop(0, HALF // 96)
        def _(i):
            rows = pl.ds(pl.multiple_of(i * 96, 16), 96)
            rest[rows, :] = out_stage[rows, :].astype(BF)

    @pl.when(s % 2 == 1)
    def _():
        for copy in odd:
            copy.wait()
        for i in range(3):
            for j in range(6):
                block = wide[j * 128 : (j + 1) * 128, FRONT + i * 128 : FRONT + (i + 1) * 128]
                rest[i * 128 : (i + 1) * 128, j * 128 : (j + 1) * 128] = block.T.astype(BF)

    @pl.loop(0, D // 96)
    def _(i):
        rows = pl.ds(pl.multiple_of(i * 96, 16), 96)
        first[rows, :] = wide[rows, 0:FRONT].astype(BF)

    tail.wait()

    quarter = D // 4
    firsts = [(first, first_all, i * quarter, quarter, i < 2) for i in range(4)]
    seconds = [(rest, rest_all, i * 192, 192, i == 0) for i in range(2)]
    small = [
        (rest, rest_all, FRONT, EXTRA, True),
        (vec_ref, vec_all, 0, 8, False),
    ]
    if spread:
        share = D // layers
        at = pl.multiple_of(HALF + z * share, 16)
        half = share // 2
        slices = [
            (rest, rest_all, at, half, True),
            (rest, rest_all, pl.multiple_of(at + half, 16), share - half, False),
        ]
    else:
        slices = [(rest, rest_all, HALF + i * 192, 192, i < 2) for i in range(4)]
    pieces = slices + firsts + seconds + small

    def part(n, ref):
        unused, unused, row, rows, unused = pieces[n]
        return ref.at[pl.ds(row, rows), :]

    def remote(n, kind, src, dst, to):
        return pltpu.make_async_remote_copy(
            src_ref=src,
            dst_ref=dst,
            send_sem=send_sem.at[kind, n],
            recv_sem=recv_sem.at[kind, n],
            device_id=(to, b),
            device_id_type=MESH,
        )

    def direct(n, kind):
        mine, every = pieces[n][:2]
        return remote(n, kind, part(n, mine), part(n, every.at[s]), y if kind else x)

    def arrived(n, kind):
        every = pieces[n][1]
        owner = (x, y, xy)[kind]
        here = part(n, every.at[owner])
        remote(n, kind, here, here, x).wait_recv()

    def relay(n):
        every, by_x = pieces[n][1], pieces[n][4]
        source = part(n, every.at[x if by_x else y])
        return remote(n, 2, source, source, y if by_x else x)

    def pass_on(n):
        arrived(n, 0 if pieces[n][4] else 1)
        relay(n).start()

    count = len(pieces)
    by_x = [n for n in range(count) if pieces[n][4]]
    by_y = [n for n in range(count) if not pieces[n][4]]
    small_n = list(range(count - 2, count))

    def early(n):
        direct(n, 0 if pieces[n][4] else 1).start()

    def late(n):
        direct(n, 1 if pieces[n][4] else 0).start()

    own = [
        pltpu.make_async_copy(first, first_all.at[s], own_sem.at[0]),
        pltpu.make_async_copy(rest, rest_all.at[s], own_sem.at[1]),
        pltpu.make_async_copy(vec_ref, vec_all.at[s], own_sem.at[2]),
    ]

    z_width = D // layers if spread else 0

    def z_part(section, owner_z):
        at = pl.multiple_of(HALF + owner_z * z_width, 16)
        return rest_all.at[section, pl.ds(at, z_width), :]

    def z_copy(way, step, k, owner_z, to_b):
        source = z_part((x, y, xy)[k], owner_z)
        return pltpu.make_async_remote_copy(
            src_ref=source,
            dst_ref=source,
            send_sem=z_send.at[way, step, k],
            recv_sem=z_recv.at[way, step, k],
            device_id=(s, to_b),
            device_id_type=MESH,
        )

    def z_first(k):
        @pl.when(z < layers - 1)
        def _():
            z_copy(0, 0, k, z, b + 2).start()

        @pl.when(z > 0)
        def _():
            z_copy(1, 0, k, z, b - 2).start()

    def z_step(step):
        @pl.when(z >= step)
        def _():
            for k in range(3):
                z_copy(0, step - 1, k, z - step, b).wait_recv()

                @pl.when(z < layers - 1)
                def _():
                    z_copy(0, step, k, z - step, b + 2).start()

        @pl.when(z < layers - step)
        def _():
            for k in range(3):
                z_copy(1, step - 1, k, z + step, b).wait_recv()

                @pl.when(z > 0)
                def _():
                    z_copy(1, step, k, z + step, b - 2).start()

    def z_drain():
        for step in range(layers - 1):

            @pl.when((z < layers - 1) & (z >= step))
            def _():
                for k in range(3):
                    z_copy(0, step, k, z - step, b + 2).wait_send()

            @pl.when((z > 0) & (z + step < layers))
            def _():
                for k in range(3):
                    z_copy(1, step, k, z + step, b - 2).wait_send()

    queue_x = [n for n in by_x]
    queue_y = [n for n in by_y]
    for n in queue_x[:2] + queue_y[:2]:
        early(n)
    for copy in own:
        copy.start()

    @pl.when(mine)
    def _():
        own_quarter.wait()
        quarter_to_twin(3, s).start()
        for i, owner in enumerate((x, y, xy)):
            feature(i, 0, owner, x).wait_recv()
            quarter_to_twin(4 + i, owner).start()
    rounds = max(len(queue_x), len(queue_y))
    late_x, late_y = list(queue_y), list(queue_x)
    z_at = 1
    for i in range(rounds):
        for queue in (queue_x, queue_y):
            if i < len(queue):
                pass_on(queue[i])
                if i + 2 < len(queue):
                    early(queue[i + 2])
                else:
                    other = late_x if queue is queue_x else late_y
                    if other:
                        late(other.pop(0))
        if spread and i == 0:
            for n, kind in ((0, 1), (1, 0)):
                late(n)
                (late_x if kind == 0 else late_y).remove(n)
        if spread and i == 1:
            arrived(0, 1)
            arrived(1, 0)
            z_first(0)
            z_first(1)
            arrived(0, 2)
            arrived(1, 2)
            z_first(2)
        if spread and i >= 2 and z_at < layers - 1:
            z_step(z_at)
            z_at += 1
    for n in late_x + late_y:
        late(n)
    done = set()
    if spread:
        done = {(0, 1), (1, 0), (0, 2), (1, 2)}
        while z_at < layers:
            z_step(z_at)
            z_at += 1
    for n in range(count):
        for kind in range(3):
            if kind == 2 or kind == (1 if pieces[n][4] else 0):
                if (n, kind) not in done:
                    arrived(n, kind)
    for n in range(count):
        direct(n, 0).wait_send()
        direct(n, 1).wait_send()
        relay(n).wait_send()
    if spread:
        z_drain()
    for copy in own:
        copy.wait()
    swap_ints.wait()

    @pl.when(mine)
    def _():
        feature(1, 1 - micro, s, y).wait_send()
        for i, owner in enumerate((s, x, y, xy)):
            quarter_to_twin(3 + i, owner).wait_send()

    @pl.when(jnp.logical_not(mine))
    def _():
        feature(0, micro, s, x).wait_send()
        feature(2, 1 - micro, s, xy).wait_send()
        for i, owner in enumerate((s, x, y, xy)):
            quarter_to_twin(3 + i, owner).wait_recv()


def fetch_weights(w, down, tail, vec, slices, ints, layers):
    spread = layers > 1 and D % (32 * layers) == 0
    anywhere = pl.BlockSpec(memory_space=pl.ANY)
    pieces = 12 if not spread else 10
    steps = max(layers - 1, 1) if spread else 1
    return pl.pallas_call(
        partial(fetch_kernel, layers, spread),
        in_specs=[anywhere] * 6,
        out_specs=[anywhere] * 5,
        out_shape=[
            jax.ShapeDtypeStruct((4, D, FRONT), BF),
            jax.ShapeDtypeStruct((4, FRONT + EXTRA, D), BF),
            jax.ShapeDtypeStruct((4, 8, D), F32),
            jax.ShapeDtypeStruct((4,) + slices.shape[1:], BF),
            jax.ShapeDtypeStruct(ints.shape, jnp.int32),
        ],
        scratch_shapes=[
            pltpu.VMEM((D, 2 * D), F32),
            pltpu.VMEM((HALF, D), F32),
            pltpu.VMEM((D, D), F32),
            pltpu.VMEM((D, FRONT), BF),
            pltpu.VMEM((FRONT + EXTRA, D), BF),
            pltpu.SemaphoreType.DMA((15,)),
            pltpu.SemaphoreType.DMA((3,)),
            pltpu.SemaphoreType.DMA((3, pieces)),
            pltpu.SemaphoreType.DMA((3, pieces)),
            pltpu.SemaphoreType.DMA((2, steps, 3)),
            pltpu.SemaphoreType.DMA((2, steps, 3)),
            pltpu.SemaphoreType.DMA((8,)),
            pltpu.SemaphoreType.DMA((8,)),
        ],
        compiler_params=pltpu.CompilerParams(
            collective_id=1, has_side_effects=True, vmem_limit_bytes=40 * 1024 * 1024
        ),
    )(w, down, tail, vec, slices, ints)


TAIL = 48
SIDE = HALF + TAIL
STREAMS = ((D, FRONT, 32, True), (SIDE, D, 16, True), (D, D, 32, False))
CHUNKS = tuple(rows // step for rows, unused, step, unused2 in STREAMS)
ONE_LOW, ONE_HIGH, TWO, INWARD, BACK, TWIN = 0, 3, 6, 9, 12, 15


def backward_kernel(layers, lags, *refs):
    hs, xhats, scales = refs[0:4], refs[4:8], refs[8:12]
    qkvs, ctxs, lses, acts, slopes = refs[12:14], refs[14:16], refs[16:18], refs[18:20], refs[20:22]
    first_all, rest_all, tails, bound_ref, vec_ref, dw_ref = refs[22:28]
    outs, out_back = refs[28:31], refs[31]
    sums, ones, twos, ins, backs = refs[32:35], refs[35:38], refs[38:41], refs[41:44], refs[44:47]
    (
        h_f,
        xhat_f,
        scale_f,
        slope,
        up_first,
        up_second,
        act_ring,
        down_ring,
        h_a,
        xhat_a,
        scale_a,
        qkv,
        ctx,
        lse,
        att_first,
        att_second,
        proj,
        dy,
        dc,
        part_out,
        part_in,
        shares,
        load_sem,
        ring_sem,
        part_send,
        part_recv,
        send_sem,
        recv_sem,
        keep_sem,
        in_send,
        in_recv,
    ) = refs[47:]
    s, b, x, y, xy = neighbours()
    z, core = b // 2, b % 2
    half = s // 2
    parity = s % 2
    mine = core == parity
    twin = b + 1 - 2 * core
    middle = max(layers // 2 - 1, 0)
    upper = z // max(layers // 2, 1)
    depth = z + upper * (layers - 1 - 2 * z)
    toward = b + 2 - 4 * upper
    outward = b - 2 + 4 * upper
    lag_z, lag_step = lags

    def load(src, dst, i):
        return pltpu.make_async_copy(src, dst, load_sem.at[i])

    def loads_ffn(l):
        t = 2 * l + 1
        return [
            load(hs[t], h_f, 0),
            load(xhats[t], xhat_f, 1),
            load(scales[t], scale_f, 2),
            load(slopes[l], slope, 3),
            load(first_all.at[t], up_first, 4),
            load(rest_all.at[t, pl.ds(0, HALF), :], up_second, 5),
        ]

    def loads_attention(l):
        t = 2 * l
        return [
            load(hs[t], h_a, 6),
            load(xhats[t], xhat_a, 7),
            load(scales[t], scale_a, 8),
            load(qkvs[l], qkv, 9),
            load(ctxs[l], ctx, 10),
            load(lses[l], lse, 11),
            load(first_all.at[t], att_first, 12),
            load(rest_all.at[t, pl.ds(0, HALF), :], att_second, 13),
        ]

    def ring(l, j):
        slot = j % 2
        rows = pl.ds(HALF + (j % 2) * HALF, HALF)
        return (
            pltpu.make_async_copy(
                acts[l].at[:, pl.ds(j * HALF, HALF)], act_ring.at[slot], ring_sem.at[0, slot]
            ),
            pltpu.make_async_copy(
                rest_all.at[2 * l + j // 2, rows, :], down_ring.at[slot], ring_sem.at[1, slot]
            ),
        )

    def start(copies):
        for copy in copies:
            copy.start()

    def wait(copies):
        for copy in copies:
            copy.wait()

    start_loads = [
        load(rest_all.at[t, pl.ds(FRONT, EXTRA), :], proj.at[pl.ds(t * EXTRA, EXTRA), :], 14 + t)
        for t in range(4)
    ] + [load(tails.at[t], sums[1].at[t, pl.ds(HALF, TAIL), :], 18 + t) for t in range(4)]
    start(start_loads)
    start(loads_ffn(1))
    start(ring(1, 0))
    start(ring(1, 1))
    start(loads_attention(1))
    greet(layers)
    wait(start_loads)

    def remote(kind, chunk, src, dst, to):
        return pltpu.make_async_remote_copy(
            src_ref=src,
            dst_ref=dst,
            send_sem=send_sem.at[kind, chunk],
            recv_sem=recv_sem.at[kind, chunk],
            device_id=to,
            device_id_type=MESH,
        )

    def rows_of(which, chunk):
        size = STREAMS[which][2]
        return pl.ds(pl.multiple_of(chunk * size, 16), size)

    def one(which, chunk, l):
        rows = rows_of(which, chunk)
        kind = (ONE_HIGH if l else ONE_LOW) + which
        if STREAMS[which][3]:
            src = sums[which].at[2 * l + 1 - parity, rows, :]
            return remote(kind, chunk, src, ones[which].at[l, rows, :], (x, b))
        src = sums[which].at[2 * (1 - half) + l, rows, :]
        return remote(kind, chunk, src, ones[which].at[l, rows, :], (y, b))

    def forwarded(which):
        return 2 * (1 - half) + parity if STREAMS[which][3] else 2 * half + 1 - parity

    def two(which, chunk):
        rows = rows_of(which, chunk)
        src = sums[which].at[forwarded(which), rows, :]
        to = y if STREAMS[which][3] else x
        return remote(TWO + which, chunk, src, twos[which].at[rows, :], (to, b))

    def inward(which, chunk, swap):
        rows = rows_of(which, chunk)
        src = sums[which].at[s, rows, :]
        if swap:
            return remote(BACK + which, chunk, src, backs[which].at[rows, :], (s, toward))
        return remote(INWARD + which, chunk, src, ins[which].at[rows, :], (s, toward))

    def final(which, at_middle):
        return sums[which].at[s] if at_middle else backs[which]

    def outward_copy(which, chunk, at_middle):
        rows = rows_of(which, chunk)
        src = final(which, at_middle).at[rows, :]
        return remote(BACK + which, chunk, src, backs[which].at[rows, :], (s, outward))

    def twin_copy(which, chunk, at_middle):
        rows = rows_of(which, chunk)
        src = final(which, at_middle).at[rows, :]
        return remote(TWIN + which, chunk, src, outs[which].at[core, rows, :], (s, twin))

    def keep_copy(which, chunk, at_middle):
        rows = rows_of(which, chunk)
        src = final(which, at_middle).at[rows, :]
        return pltpu.make_async_copy(
            src, outs[which].at[core, rows, :], keep_sem.at[which, chunk]
        )

    def plus(*values):
        total = values[0].astype(F32)
        for value in values[1:]:
            total = total + value.astype(F32)
        return total

    def send_x_first(which, l, start_row, rows):
        size = STREAMS[which][2]

        def body(c, unused):
            one(which, c, l).start()
            return unused

        lax.fori_loop(start_row // size, (start_row + rows) // size, body, 0)

    def send_y_first(which, layer, p, start_row, rows):
        size = STREAMS[which][2]

        @pl.when(half != layer)
        def _():
            def body(c, unused):
                one(which, c, p).start()
                return unused

            lax.fori_loop(start_row // size, (start_row + rows) // size, body, 0)

    def swap_copy(t, i):
        rows = pl.ds(i * 256, 256)
        return pltpu.make_async_remote_copy(
            src_ref=part_out.at[rows, :],
            dst_ref=part_in.at[t % 2, rows, :],
            send_sem=part_send.at[t, i],
            recv_sem=part_recv.at[t, i],
            device_id=(s, twin),
            device_id_type=MESH,
        )

    def norm_back(t, grad_of, xhat, scale):
        gain = vec_ref[t, 1:2, :]

        def body(i, carry):
            rows = pl.ds(pl.multiple_of(i * 128, 128), 128)
            grad = grad_of(rows)
            xh = xhat[rows, :].astype(F32)
            weighted = grad * gain
            mean_1 = jnp.mean(weighted, -1, keepdims=True)
            mean_2 = jnp.mean(weighted * xh, -1, keepdims=True)
            du = scale[rows, 0:1] * (weighted - mean_1 - xh * mean_2)
            dy[rows, :] = du.astype(BF)
            return (
                carry[0] + jnp.sum(du, 0, keepdims=True),
                carry[1] + jnp.sum(grad * xh, 0, keepdims=True),
                carry[2] + jnp.sum(grad, 0, keepdims=True),
            )

        zero = jnp.zeros((1, D), F32)
        carry = (zero, zero, zero)
        for i in range(3):
            if t < 3:
                swap_copy(t + 1, i).wait_recv()
            carry = lax.fori_loop(2 * i, 2 * i + 2, body, carry)
        row = lax.broadcasted_iota(jnp.int32, (16, 1), 0)
        block = sums[1][t, HALF : HALF + 16, :].astype(F32)
        for i in range(3):
            block = jnp.where(row == i, carry[i], block)
        sums[1][t, HALF : HALF + 16, :] = block.astype(BF)

    def grad_from_head(rows):
        return mm(dw_ref[rows, :], proj[...])

    def grad_from(t):
        def grad_of(rows):
            total = plus(dy[rows, :], part_out[rows, :], part_in[t % 2, rows, :])
            return total.astype(BF).astype(F32)

        return grad_of

    def ffn_back(l):
        t = 2 * l + 1
        for j in range(4):
            wait(ring(l, j))
            slot = j % 2
            columns = slice(j * HALF, (j + 1) * HALF)
            low = dy[...]
            to = (j % 2) * HALF
            sums[2][2 * l + j // 2, to : to + HALF, :] = mm(
                act_ring[slot], low, ((0,), (0,))
            ).astype(BF)
            send_y_first(2, l, j // 2, to, HALF)
            for i in range(3):
                rows = slice(i * 256, (i + 1) * 256)
                grad = mm(dy[rows, :], down_ring[slot], ((1,), (1,)))
                slope[rows, columns] = (grad * slope[rows, columns].astype(F32)).astype(BF)
            if j < 2:
                start(ring(l, j + 2))
        for i in range(3):
            rows = slice(i * 256, (i + 1) * 256)
            if t < 3:
                swap_copy(t + 1, i).wait_send()
            part = mm(slope[rows, 0:FRONT], up_first[...], ((1,), (1,)))
            part = part + mm(slope[rows, FRONT:], up_second[...])
            part_out[rows, :] = part.astype(BF)
            swap_copy(t, i).start()
        for i in range(3):
            rows = slice(i * 256, (i + 1) * 256)
            sums[0][t, rows, :] = mm(h_f[:, rows], slope[:, 0:FRONT], ((0,), (0,))).astype(BF)
        sums[1][t, 0:HALF, :] = mm(slope[:, FRONT:], h_f[...], ((0,), (0,))).astype(BF)

    def attention_pair(i, unused):
        lane = lax.broadcasted_iota(jnp.int32, (1, 128), 1)
        base = pl.multiple_of(i * 384, 128)
        q_at, k_at, v_at = (
            pl.ds(base, 128),
            pl.ds(pl.multiple_of(base + 128, 128), 128),
            pl.ds(pl.multiple_of(base + 256, 128), 128),
        )
        c_at = pl.ds(pl.multiple_of(i * 128, 128), 128)
        for which, (begin, size) in enumerate(BLOCKS):
            chunk = min(size, 256)
            span = slice(begin, begin + size)
            k = qkv[span, k_at]
            v = qkv[span, v_at]
            dk = jnp.zeros((size, 128), F32)
            dv = jnp.zeros((size, 128), F32)
            for at in range(begin, begin + size, chunk):
                rows = slice(at, at + chunk)
                q = qkv[rows, q_at]
                dcs = dc[rows, c_at]
                dq = None
                for head in range(2):
                    own = (lane < 64) if head == 0 else (lane >= 64)
                    qm = jnp.where(own, q, jnp.zeros_like(q)) * BF(0.125)
                    dcm = jnp.where(own, dcs, jnp.zeros_like(dcs))
                    km = jnp.where(own, k, jnp.zeros_like(k))
                    score = mm(k, qm, ((1,), (1,)))
                    if which != 1:
                        score = jnp.where(block_mask(which, bound_ref[0], size), score, MASKED)
                    p = jnp.exp(score - lse[i, head : head + 1, rows])
                    dp = mm(v, dcm, ((1,), (1,)))
                    inner = jnp.sum(p * dp, axis=0, keepdims=True)
                    ds = (p * (dp - inner)).astype(BF)
                    dv = dv + mm(p.astype(BF), dcm)
                    dk = dk + mm(ds, qm)
                    part = mm(km, ds, ((0,), (0,)))
                    dq = part if dq is None else dq + part
                qkv[rows, q_at] = (dq.T * 0.125).astype(BF)
            qkv[span, k_at] = dk.astype(BF)
            qkv[span, v_at] = dv.astype(BF)
        return unused

    def attention_grads(l):
        t = 2 * l
        sums[1][t, 0:HALF, :] = mm(ctx[...], dy[...], ((0,), (0,))).astype(BF)
        for i in range(3):
            rows = slice(i * 256, (i + 1) * 256)
            dc[rows, :] = mm(dy[rows, :], att_second[...], ((1,), (1,))).astype(BF)
        lax.fori_loop(0, PAIRS, attention_pair, 0)
        for i in range(3):
            rows = slice(i * 256, (i + 1) * 256)
            swap_copy(t + 1, i).wait_send()
            part_out[rows, :] = mm(qkv[rows, :], att_first[...], ((1,), (1,))).astype(BF)
            swap_copy(t, i).start()
        for i in range(3):
            rows = slice(i * 256, (i + 1) * 256)
            sums[0][t, rows, :] = mm(h_a[:, rows], qkv[...], ((0,), (0,))).astype(BF)

    def start_x_first(t):
        l, p = t // 2, t % 2

        @pl.when(parity != p)
        def _():
            for which in (1, 0):
                send_x_first(which, l, 0, STREAMS[which][0])

    wait(loads_ffn(1))
    norm_back(3, grad_from_head, xhat_f, scale_f)
    ffn_back(1)
    start_x_first(3)
    start(loads_ffn(0))
    start(ring(0, 0))
    start(ring(0, 1))
    wait(loads_attention(1))
    norm_back(2, grad_from(3), xhat_a, scale_a)
    attention_grads(1)
    start_x_first(2)
    start(loads_attention(0))
    wait(loads_ffn(0))
    norm_back(1, grad_from(2), xhat_f, scale_f)
    ffn_back(0)
    start_x_first(1)
    wait(loads_attention(0))
    norm_back(0, grad_from(1), xhat_a, scale_a)
    attention_grads(0)
    start_x_first(0)

    width = shares.shape[2]
    for i in range(3):
        swap_copy(0, i).wait_recv()

        def body(j, unused):
            rows = pl.ds(pl.multiple_of(j * 64, 64), 64)
            total = plus(dy[rows, :], part_out[rows, :], part_in[0, rows, :])
            for f in range(4):
                shares[f, rows, :] = total[:, f * width : (f + 1) * width].astype(BF)
            return unused

        lax.fori_loop(4 * i, 4 * i + 4, body, 0)

    def back_to(i, to):
        return pltpu.make_async_remote_copy(
            src_ref=shares.at[to],
            dst_ref=out_back.at[i],
            send_sem=in_send.at[i],
            recv_sem=in_recv.at[i],
            device_id=(to, b),
            device_id_type=MESH,
        )

    own_share = pltpu.make_async_copy(shares.at[s], out_back.at[3], in_send.at[3])
    own_share.start()

    @pl.when(mine)
    def _():
        for i, to in enumerate((x, y, xy)):
            back_to(i, to).start()

    def came_one(which, chunk, l):
        one(which, chunk, l).wait_recv()

    def start_two(which, chunk):
        rows = rows_of(which, chunk)
        t = forwarded(which)
        if STREAMS[which][3]:
            came_one(which, chunk, 0)
            came_one(which, chunk, 1)
            got = ones[which][1 - half, rows, :]
        else:
            came_one(which, chunk, 0)
            came_one(which, chunk, 1)
            got = ones[which][1 - parity, rows, :]
        sums[which][t, rows, :] = plus(sums[which][t, rows, :], got).astype(BF)
        two(which, chunk).start()

    def start_z(which, chunk):
        rows = rows_of(which, chunk)
        two(which, chunk).wait_recv()
        got = ones[which][half if STREAMS[which][3] else parity, rows, :]
        total = plus(sums[which][s, rows, :], got, twos[which][rows, :])
        if layers == 1:
            sums[which][s, rows, :] = total.astype(BF)
            twin_copy(which, chunk, True).start()
            keep_copy(which, chunk, True).start()
            return
        if middle > 0:

            @pl.when(depth > 0)
            def _():
                inward(which, chunk, False).wait_recv()
                sums[which][s, rows, :] = plus(total, ins[which][rows, :]).astype(BF)

            @pl.when(depth == 0)
            def _():
                sums[which][s, rows, :] = total.astype(BF)

            @pl.when(depth < middle)
            def _():
                inward(which, chunk, False).start()

        else:
            sums[which][s, rows, :] = total.astype(BF)

        @pl.when(depth == middle)
        def _():
            inward(which, chunk, True).start()

    def finish(which, chunk):
        rows = rows_of(which, chunk)
        inward(which, chunk, True).wait_recv()

        @pl.when(depth == middle)
        def _():
            inward(which, chunk, True).wait_send()
            sums[which][s, rows, :] = plus(
                sums[which][s, rows, :], backs[which][rows, :]
            ).astype(BF)
            if middle > 0:
                outward_copy(which, chunk, True).start()
            twin_copy(which, chunk, True).start()
            keep_copy(which, chunk, True).start()

        if middle > 0:

            @pl.when(depth < middle)
            def _():
                @pl.when(depth > 0)
                def _():
                    outward_copy(which, chunk, False).start()

                twin_copy(which, chunk, False).start()
                keep_copy(which, chunk, False).start()

    lag3 = lag_z + lag_step * depth
    lag5 = lag_z + lag_step * (middle + 1) + lag_step * (middle - depth)
    slots = max(CHUNKS) + lag_z + (lag_step * (2 * middle + 1) if layers > 1 else 0)

    def guarded(chunk, step):
        for which, count in enumerate(CHUNKS):

            @pl.when((chunk >= 0) & (chunk < count))
            def _():
                step(which, chunk)

    def slot(k, unused):
        guarded(k, start_two)
        guarded(k - lag3, start_z)
        if layers > 1:
            guarded(k - lag5, finish)
        return unused

    lax.fori_loop(0, slots, slot, 0)

    def drain(which, chunk):
        twin_copy(which, chunk, True).wait_recv()
        twin_copy(which, chunk, True).wait_send()
        keep_copy(which, chunk, True).wait()
        if STREAMS[which][3]:
            one(which, chunk, 0).wait_send()
            one(which, chunk, 1).wait_send()
        else:
            one(which, chunk, 0).wait_send()
            one(which, chunk, 1).wait_send()
        two(which, chunk).wait_send()
        if layers > 1 and middle > 0:

            @pl.when(depth < middle)
            def _():
                inward(which, chunk, False).wait_send()

            @pl.when(depth > 0)
            def _():
                outward_copy(which, chunk, True).wait_send()

    def last(k, unused):
        guarded(k, drain)
        return unused

    lax.fori_loop(0, max(CHUNKS), last, 0)
    for i in range(3):
        swap_copy(0, i).wait_send()
    own_share.wait()

    @pl.when(mine)
    def _():
        for i, to in enumerate((x, y, xy)):
            back_to(i, to).wait_send()
        back_to(1, y).wait_recv()

    @pl.when(jnp.logical_not(mine))
    def _():
        back_to(0, x).wait_recv()
        back_to(2, xy).wait_recv()


def backward(hs, xhats, scales, kept, first_all, rest_all, tails, bound, vec, dw, width, layers, lags=(1, 1)):
    anywhere = pl.BlockSpec(memory_space=pl.ANY)
    inside = pl.BlockSpec(memory_space=pltpu.VMEM)
    shapes = [(rows, columns) for rows, columns, unused, unused2 in STREAMS]
    most = max(CHUNKS)
    return pl.pallas_call(
        partial(backward_kernel, layers, lags),
        in_specs=[anywhere] * 25
        + [pl.BlockSpec(memory_space=pltpu.SMEM), inside, inside],
        out_specs=[anywhere] * 4,
        out_shape=[jax.ShapeDtypeStruct((2,) + shape, BF) for shape in shapes]
        + [jax.ShapeDtypeStruct((4, ROWS, width), BF)],
        scratch_shapes=[pltpu.VMEM((4,) + shape, BF) for shape in shapes]
        + [pltpu.VMEM((2,) + shape, BF) for shape in shapes]
        + [pltpu.VMEM(shape, BF) for shape in shapes] * 3
        + [
            pltpu.VMEM((ROWS, D), BF),
            pltpu.VMEM((ROWS, D), BF),
            pltpu.VMEM((ROWS, 128), F32),
            pltpu.VMEM((ROWS, 2 * D), BF),
            pltpu.VMEM((D, FRONT), BF),
            pltpu.VMEM((HALF, D), BF),
            pltpu.VMEM((2, ROWS, HALF), BF),
            pltpu.VMEM((2, HALF, D), BF),
            pltpu.VMEM((ROWS, D), BF),
            pltpu.VMEM((ROWS, D), BF),
            pltpu.VMEM((ROWS, 128), F32),
            pltpu.VMEM((ROWS, FRONT), BF),
            pltpu.VMEM((ROWS, HALF), BF),
            pltpu.VMEM((PAIRS, 8, ROWS), F32),
            pltpu.VMEM((D, FRONT), BF),
            pltpu.VMEM((HALF, D), BF),
            pltpu.VMEM((4 * EXTRA, D), BF),
            pltpu.VMEM((ROWS, D), BF),
            pltpu.VMEM((ROWS, HALF), BF),
            pltpu.VMEM((ROWS, D), BF),
            pltpu.VMEM((2, ROWS, D), BF),
            pltpu.VMEM((4, ROWS, width), BF),
            pltpu.SemaphoreType.DMA((22,)),
            pltpu.SemaphoreType.DMA((2, 2)),
            pltpu.SemaphoreType.DMA((4, 3)),
            pltpu.SemaphoreType.DMA((4, 3)),
            pltpu.SemaphoreType.DMA((18, most)),
            pltpu.SemaphoreType.DMA((18, most)),
            pltpu.SemaphoreType.DMA((3, most)),
            pltpu.SemaphoreType.DMA((4,)),
            pltpu.SemaphoreType.DMA((4,)),
        ],
        compiler_params=pltpu.CompilerParams(
            collective_id=2, has_side_effects=True, vmem_limit_bytes=62 * 1024 * 1024
        ),
    )(*hs, *xhats, *scales, *kept, first_all, rest_all, tails, bound, vec, dw)


def assemble_kernel(first_ref, rest_ref, out_ref):
    is_ffn = lax.axis_index("section") % 2
    row = pl.program_id(0)

    @pl.when(is_ffn == 0)
    def _():
        for core in range(2):
            for i in range(PAIRS):
                for t in range(3):
                    to = t * D + core * HALF + i * 128
                    at = (3 * i + t) * 128
                    out_ref[:, to : to + 128] = first_ref[core, :, at : at + 128].astype(F32)
        from_core = row // 3
        at = pl.multiple_of((row % 3) * 128, 128)
        out_ref[:, 3 * D :] = rest_ref[from_core, pl.ds(at, 128), :].astype(F32)

    @pl.when(is_ffn == 1)
    def _():
        lanes = pl.ds(pl.multiple_of(row * 128, 128), 128)
        for core in range(2):
            out_ref[:, core * D : (core + 1) * D] = first_ref[core, :, 0:D].astype(F32)
            at = 2 * D + core * D
            out_ref[:, at : at + HALF] = first_ref[core, :, D:].astype(F32)
            out_ref[:, at + HALF : at + D] = rest_ref[core, 0:HALF, lanes].astype(F32).T


def assemble(first_sum, rest_sum):
    return pl.pallas_call(
        assemble_kernel,
        grid=(D // 128,),
        in_specs=[
            pl.BlockSpec((2, 128, FRONT), lambda i: (0, i, 0)),
            pl.BlockSpec((2, SIDE, D), lambda i: (0, 0, 0)),
        ],
        out_specs=pl.BlockSpec((128, 4 * D), lambda i: (i, 0)),
        out_shape=jax.ShapeDtypeStruct((D, 4 * D), F32),
        compiler_params=pltpu.CompilerParams(vmem_limit_bytes=32 * 1024 * 1024),
    )(first_sum, rest_sum)


def layer_norm(residual, gain, shift):
    row_mean = jnp.mean(residual, -1, keepdims=True)
    centered = residual - row_mean
    return (
        centered * lax.rsqrt(jnp.mean(centered * centered, -1, keepdims=True) + NORM_EPSILON) * gain
        + shift
    )


def normalize(projected):
    return projected * lax.rsqrt(jnp.sum(projected * projected, -1, keepdims=True) + NORM_EPSILON)


def gelu_and_slope(z):
    upper = 0.5 * (1.0 + lax.erf(z * 0.7071067811865476))
    density = jnp.exp(-0.5 * z * z) * 0.3989422804014327
    return (z * upper).astype(BF), (upper + z * density).astype(BF)


def maxsim_loss(affinity, valid, positive):
    logits = jnp.where(valid[None, :, :], affinity[:, None, :] / SOFTMAX_DIVISOR, MASKED)
    soft = SOFTMAX_DIVISOR * jax.nn.logsumexp(logits, -1)
    scores = jnp.sum(soft.reshape(QUERY_COUNT, QUERY_LENGTH, -1), 1) * SIMILARITY_SCALE
    choose = jnp.arange(scores.shape[1], dtype=jnp.int32)[None, :] == positive[:, None]
    picked = jnp.sum(jnp.where(choose, scores, 0.0), 1)
    return jnp.sum(jax.nn.logsumexp(scores, -1) - picked)


def on_device(
    inputs,
    in_weight,
    down_weight,
    out_bias,
    norm_gains,
    norm_shifts,
    projection,
    passage_lengths,
    positive,
):
    batches = lax.axis_size("batch")
    layers = batches // 2
    s = lax.axis_index("section")
    b = lax.axis_index("batch")
    core = b % 2
    groups = inputs.shape[0] * batches
    queries_all = groups * QUERY_COUNT

    def other_core(value):
        return lax.ppermute(value, "batch", [(j, j ^ 1) for j in range(batches)])

    def pick(table, index):
        return lax.dynamic_index_in_dim(table, index, 0, keepdims=False)

    mine = core == s % 2
    micro = s // 2
    lengths_all = passage_lengths[:, 0]

    def long_start(lengths):
        return jnp.where(
            lengths[0] == PLEN, 0, jnp.where(lengths[1] == PLEN, lengths[0], lengths[0] + lengths[1])
        )

    def rolled(rows, start):
        passages = rows[QROWS:]
        doubled = jnp.concatenate([passages, passages[:REST]], 0)
        return jnp.concatenate(
            [rows[:QROWS], lax.dynamic_slice_in_dim(doubled, start, PASSAGE_TOKENS, 0)], 0
        )

    def unrolled(rows, start):
        passages = rows[QROWS:]
        doubled = jnp.concatenate([passages[PLEN:], passages], 0)
        return jnp.concatenate(
            [rows[:QROWS], lax.dynamic_slice_in_dim(doubled, REST - start, PASSAGE_TOKENS, 0)], 0
        )

    slices = jnp.stack([rolled(inputs[m], long_start(lengths_all[m])) for m in range(2)])
    ints = jnp.pad(
        jnp.concatenate([lengths_all, positive], 1),
        ((0, 6), (0, 128 - PASSAGE_COUNT - QUERY_COUNT)),
    )
    vec = jnp.concatenate([out_bias, norm_gains, norm_shifts, jnp.zeros((5, D), F32)], 0)
    first_all, rest_all, vectors, parts_all, ints_other = fetch_weights(
        in_weight[0], down_weight, projection.T.astype(BF), vec, slices, ints, layers
    )
    packs = [
        (first_all[t], rest_all[t, :HALF], rest_all[t, HALF:FRONT]) for t in range(4)
    ]
    projector = jnp.concatenate([rest_all[t, FRONT:] for t in range(4)], 0).T
    entry = jnp.concatenate([parts_all[f] for f in range(4)], 1)
    ints = pick(jnp.where(mine, ints, ints_other), micro)
    lengths = ints[:PASSAGE_COUNT]
    chosen = ints[PASSAGE_COUNT : PASSAGE_COUNT + QUERY_COUNT]
    long_index = jnp.where(lengths[0] == PLEN, 0, jnp.where(lengths[1] == PLEN, 1, 2))
    after = (long_index + 1) % 3
    bound = pick(lengths, after)
    at = jnp.arange(PASSAGE_TOKENS, dtype=jnp.int32)
    owner = jnp.where(at < PLEN, long_index, jnp.where(at < PLEN + bound, after, (after + 1) % 3))
    valid = owner[None, :] == jnp.arange(PASSAGE_COUNT, dtype=jnp.int32)[:, None]
    bound = bound.reshape(1)

    def summed(part):
        own = part.astype(BF)
        return own.astype(F32) + other_core(own).astype(F32)

    h = entry
    hs, xhats, scales, kept = [], [], [], [[], [], [], [], []]
    for t in range(4):
        one, two, three = packs[t]
        bias, gain, shift = vectors[t, 0], vectors[t, 1], vectors[t, 2]
        if t % 2 == 0:
            qkv = mm(h, one).astype(BF)
            ctx, lse = attention(qkv, bound)
            branch = summed(mm(ctx, two))
            saved = (qkv, ctx, lse)
        else:
            down = jnp.concatenate([packs[t - 1][2], three], 0)
            z = jnp.concatenate([mm(h, one), mm(h, two, ((1,), (1,)))], 1)
            act, slope = gelu_and_slope(z)
            branch = summed(mm(act, down))
            saved = (None, None, None, act, slope)
        residual = h.astype(F32) + branch + bias
        centered = residual - jnp.mean(residual, -1, keepdims=True)
        scale = lax.rsqrt(jnp.mean(centered * centered, -1, keepdims=True) + NORM_EPSILON)
        xhat = centered * scale
        hs.append(h)
        xhats.append(xhat.astype(BF))
        scales.append(jnp.broadcast_to(scale, (ROWS, 128)))
        for i, value in enumerate(saved):
            if value is not None:
                kept[i].append(value)
        h = (xhat * gain + shift).astype(BF)

    projected = mm(h, projector)
    normed, norm_pull = jax.vjp(normalize, projected)
    embedded = normed.astype(BF)
    affinity = mm(embedded[:QROWS], embedded[QROWS:], ((1,), (1,)))
    loss, loss_pull = jax.vjp(partial(maxsim_loss, valid=valid, positive=chosen), affinity)
    left, steps = loss, []
    for unit in (8.0, 0.5, 2.0**-5, 2.0**-9, 2.0**-13, 2.0**-17):
        steps.append(jnp.floor(left / unit) * unit)
        left = left - steps[-1]
    loss_row = jnp.pad(jnp.stack(steps), (0, D - len(steps)))
    grad_sim = loss_pull(jnp.asarray(1.0 / queries_all, F32))[0].astype(BF)
    grad_embedded = jnp.concatenate(
        [mm(grad_sim, embedded[QROWS:]), mm(grad_sim, embedded[:QROWS], ((0,), (0,)))], 0
    )
    grad_projected = norm_pull(grad_embedded)[0].astype(BF)
    grad_projector = mm(h, grad_projected, ((0,), (0,)))

    columns = projection.shape[1]
    tails = jnp.stack(
        [
            jnp.concatenate(
                [
                    jnp.zeros((3, D), F32),
                    loss_row[None],
                    jnp.zeros((12, D), F32),
                    lax.slice_in_dim(grad_projector, t * columns, (t + 1) * columns, axis=1).T,
                ],
                0,
            )
            for t in range(4)
        ]
    ).astype(BF)
    first_sum, side_sum, down_sum, back = backward(
        hs,
        xhats,
        scales,
        sum(kept, []),
        first_all,
        rest_all,
        tails,
        bound,
        vectors,
        grad_projected,
        inputs.shape[2],
        layers,
    )
    in_grad = assemble(first_sum, side_sum)
    down_grad = down_sum.reshape(2 * D, D).astype(F32)
    extra = side_sum[0, HALF:].astype(F32)
    total_loss = jnp.sum(extra[3, :6]) / queries_all
    same_micro = jnp.where(mine, back[3], back[0])
    other_micro = jnp.where(mine, back[1], back[2])
    by_micro = [jnp.where(micro == m, same_micro, other_micro).astype(F32) for m in range(2)]
    input_grad = jnp.stack([unrolled(by_micro[m], long_start(lengths_all[m])) for m in range(2)])

    return (
        total_loss,
        input_grad,
        in_grad[None],
        down_grad,
        extra[0:1],
        extra[1:2],
        extra[2:3],
        extra[16:].T,
    )


def solution(mesh):
    in_specs = (
        P(None, "batch", "section"),
        P("section", None, None),
        P("section", None),
        P("section", None),
        P("section", None),
        P("section", None),
        P(None, "section"),
        P(None, "batch", None),
        P(None, "batch"),
    )
    out_specs = (
        P(),
        P(None, "batch", "section"),
        P("section", None, None),
        P("section", None),
        P("section", None),
        P("section", None),
        P("section", None),
        P(None, "section"),
    )
    return jax.shard_map(
        on_device, mesh=mesh, in_specs=in_specs, out_specs=out_specs, check_vma=False
    )
```

time: 2240 us -> 479 us (0.21)
  waiting for transfers between devices: 899 us -> 7.29 us
  Pallas kernels: 0 us -> 380 us
  other arithmetic: 343 us -> 35.7 us
  matrix products: 288 us -> 17.4 us
  loops' own time: 263 us -> 0 us
  blocking collectives: 163 us -> 0 us
  local copies, waits for them, and re-layouts: 155 us -> 22.3 us
  starting transfers between devices: 108 us -> 0.67 us
    psum x2 -> x0, waiting for transfers between devices: 430 us -> none  [the longest x1 369 us: on_device(): lax.psum((grad_in, grad_down, grad_bias, grad_gain, grad_shift), 'batch')]
    ppermute x12 -> x4, waiting for transfers between devices: 424 us -> 7.29 us  [other_core(): return lax.ppermute(value, 'batch', [(j, j ^ 1) for j in range(batches)])]
    pallas_call x0 -> x5, Pallas kernels: none -> 380 us  [the longest x1 254 us: backward(): pl.pallas_call(partial(backward_kernel, layers, lags), in_specs=[anywhere...]
    dot_general x32 -> x15, matrix products: 288 us -> 17.4 us  [mm(): return lax.dot_general(a, b, (dims, ((), ())), preferred_element_type=F32)]
    another operation x12 -> x0, loops' own time: 263 us -> none  [the longest x5 141 us: backward_tick(): lax.switch(branch_id, backward_steps, held_inputs[micro_slot], arriving.a...]
    add x30 -> x1, other arithmetic: 125 us -> 0.59 us  [on_device(): PLEN + bound]
    ppermute x12 -> x4, starting transfers between devices: 108 us -> 0.67 us  [other_core(): return lax.ppermute(value, 'batch', [(j, j ^ 1) for j in range(batches)])]
    psum x2 -> x0, blocking collectives: 103 us -> none  [the longest x1 87.8 us: on_device(): head_total = lax.psum((grad_projector, loss_sum), ('section', 'batch'))]
  transfers between devices with their start and end apart: 16 -> 4, of which waited for: 11 -> 3; matrix products, arithmetic and copies ran while one was open for 8% -> 1% of each run, Pallas kernels for 0% -> 0%
where the time goes in v1:
time: 479 us; the launch traced here: 476 us
  Pallas kernels  380 us (79%)
  other arithmetic  35.7 us (7%)
  local copies, waits for them, and re-layouts  22.3 us (5%)
  matrix products  17.4 us (4%)
  between operations  12.7 us (3%)
  waiting for transfers between devices  7.29 us (2%)
    pallas_call x1, Pallas kernels, backward(): pl.pallas_call(partial(backward_kernel, layers, lags), in_specs=[anywhere...  254 us
    pallas_call x1, Pallas kernels, fetch_weights(): pl.pallas_call(partial(fetch_kernel, layers, spread), in_specs=[anywhere]...  104 us
    dot_general x15, matrix products, mm(): return lax.dot_general(a, b, (dims, ((), ())), preferred_element_type=F32)  17.4 us
    pallas_call x2, Pallas kernels, attention(): pl.pallas_call(attention_kernel, grid=(PAIRS,), in_specs=[pl.BlockSpec(me...  17.3 us
  transfers between devices with their start and end apart: 4, of which 3 were waited for; matrix products, arithmetic and copies ran while one was open for 1% of the time, Pallas kernels for 0%

profile of v1, /device:TPU:0, one launch (start us, length us, event | category | flops | bytes accessed | tf_op | source)
XLA Modules:
  0.0 476.1 jit_solution(7913824769133033267)
XLA Ops:
  0.7 1.4 fusion.92
  4.6 0.9 fusion.90
  5.5 1.1 fusion.91
  11.5 0.6 fusion.52
  12.2 0.6 fusion.53
  13.2 2.3 copy-done.1
  15.6 104.3 %shard_map.152 = (bf16[4,768,1152]{2,1,0:T(8,128)(2,1)S(1)}, bf16[4,1184,768]{2,1,0:T(8,128)(2,1)}, f32[4,8,768]{2,1,0:T(8,128)S(1)}, bf16[4,768,192]{2,1,0:T(8,128)(2,1)S(1)}, s32[8,128]{1,0:T(8,128)S(1)}) custom-call(f32[768,3072]{1,0:T(8,128)} %bitcast.150, f32[1536,768]{1,0:T(8,128)S(1)} %copy-done.1, bf16[32,768]{1,0:T(8,128)(2,1)S(1)} %convert_bitcast_fusion.tail_ref, ...), custom_call_target="tpu_custom_call" | custom-call | tf_op jit(solution)/shard_map/pallas_call | solution.py:536
  119.9 3.0 copy-done
  122.9 0.6 fusion.93
  124.9 0.6 fusion.94
  125.5 0.5 pad_maximum_fusion.3.refs_0_
  126.0 3.7 convolution_convert_fusion.1.qkv_ref.refs_12_
  129.7 8.7 %shard_map.153 = (bf16[768,384]{1,0:T(8,128)(2,1)S(1)}, f32[3,8,768]{2,1,0:T(8,128)S(1)}) custom-call(s32[1]{0:T(128)} %bitcast.20.bound_ref.refs_25_, bf16[768,1152]{1,0:T(8,128)(2,1)S(1)} %convolution_convert_fusion.1.qkv_ref.refs_12_), custom_call_target="tpu_custom_call" | custom-call | flops 805306368 | bytes 3000000 | tf_op jit(solution)/shard_map/pallas_call | solution.py:71
  138.4 0.8 convolution_convert_fusion.3
  139.3 0.6 slice_reduce_fusion.1
  140.2 1.9 collective-permute-done
  142.1 1.0 fusion.86
  143.1 1.3 multiply_reduce_fusion.3
  144.4 2.6 multiply_convert_fusion.5
  147.1 1.7 fusion.21
  148.8 0.8 fusion.44
  149.6 3.5 fusion.4
  153.1 2.0 fusion.31
  155.3 2.7 collective-permute-done.1
  158.0 0.6 fusion.87
  158.6 0.8 multiply_reduce_fusion.2
  159.5 1.9 multiply_convert_fusion.4
  161.4 1.7 convolution_convert_fusion.qkv_ref.refs_13_
  163.1 8.7 %shard_map.154 = (bf16[768,384]{1,0:T(8,128)(2,1)S(1)}, f32[3,8,768]{2,1,0:T(8,128)S(1)}) custom-call(s32[1]{0:T(128)} %bitcast.20.bound_ref.refs_25_, bf16[768,1152]{1,0:T(8,128)(2,1)S(1)} %convolution_convert_fusion.qkv_ref.refs_13_), custom_call_target="tpu_custom_call" | custom-call | flops 805306368 | bytes 3000000 | tf_op jit(solution)/shard_map/pallas_call | solution.py:71
  171.8 0.8 convolution_convert_fusion.2
  172.8 2.7 collective-permute-done.2
  175.5 0.6 fusion.88
  176.2 0.8 multiply_reduce_fusion.1
  177.0 1.9 multiply_convert_fusion.3
  178.9 1.7 fusion.18
  180.6 0.8 fusion.41
  181.4 3.4 fusion.9
  184.7 2.0 fusion.28
  187.0 0.6 pad.36.clone
  187.5 0.7 pad.38.clone
  188.2 0.6 select_select_fusion
  188.9 0.6 slice_bitcast_fusion.26
  189.4 0.6 iota_compare_fusion
  190.0 0.9 slice_bitcast_fusion.22
  190.9 0.6 fusion.89
  191.5 0.8 multiply_reduce_fusion
  192.4 1.9 add_convert_fusion
  194.3 0.6 multiply_reduce_fusion.5
  194.8 0.5 copy-done.17
  196.7 0.6 fusion.79
  200.8 0.8 pad_maximum_fusion.6.refs_24_
  201.5 0.9 broadcast_in_dim.107.refs_11_
  202.5 0.9 broadcast_in_dim.106.refs_10_
  203.4 0.9 broadcast_in_dim.105.refs_9_
  204.3 0.9 broadcast_in_dim.104.refs_8_
  205.2 253.9 %shard_map.155 = (bf16[2,768,1152]{2,1,0:T(8,128)(2,1)}, bf16[2,432,768]{2,1,0:T(8,128)(2,1)}, bf16[2,768,768]{2,1,0:T(8,128)(2,1)}, bf16[4,768,192]{2,1,0:T(8,128)(2,1)}) custom-call(bf16[768,768]{1,0:T(8,128)(2,1)} %copy-done.16, bf16[768,768]{1,0:T(8,128)(2,1)} %copy-done.12, bf16[768,768]{1,0:T(8,128)(2,1)} %copy-done.13, bf16[768,768]{1,0:T(8,128)(2,1)} %copy-done.11, ...), custom_call_target="tpu_custom_call" | custom-call | tf_op jit(solution)/shard_map/pallas_call | solution.py:1113
  459.1 1.6 select_convert_fusion.1
  460.9 0.6 slice_bitcast_fusion.14
  461.5 0.6 slice_bitcast_fusion.23
  462.1 0.6 copy-done.2
  462.8 4.6 shard_map.156
  467.8 1.5 copy.51
  469.2 4.2 bitcast_convert_fusion
  473.5 0.6 slice_reduce_fusion.12
  (147 shorter events, 6.5 us)
Async XLA Ops:
  0.6 10.7 %copy-start.26 = (s32[2,1,3]{2,1,0:T(1,128)S(1)}, s32[2,1,3]{2,1,0:T(1,128)}, u32[]{:S(2)}) copy-start(s32[2,1,3]{2,1,0:T(1,128)} %param.16) | copy-start | bytes 76
  0.6 10.7 %copy-start.31 = (s32[2,4]{1,0:T(2,128)S(1)}, s32[2,4]{1,0:T(2,128)}, u32[]{:S(2)}) copy-start(s32[2,4]{1,0:T(2,128)} %param.17) | copy-start | bytes 100
  0.7 10.8 %copy-start.20 = (f32[768,32]{0,1:T(8,128)S(1)}, f32[768,32]{0,1:T(8,128)}, u32[]{:S(2)}) copy-start(f32[768,32]{0,1:T(8,128)} %param.15) | copy-start | bytes 294916
  11.5 1.7 copy-start.27
  11.5 1.7 copy-start.28
  11.5 1.7 copy-start.29
  13.2 2.3 copy-start.1
  119.9 3.0 copy-start
  122.8 16.4 %copy-start.8 = (f32[4,8,768]{2,1,0:T(8,128)}, f32[4,8,768]{2,1,0:T(8,128)S(1)}, u32[]{:S(2)}) copy-start(f32[4,8,768]{2,1,0:T(8,128)S(1)} %get-tuple-element.26.refs_26_) | copy-start | bytes 294916
  126.0 3.7 copy-start.16
  126.0 12.4 %slice-start.2 = ((s8[7274496]{0:T(1024)(128)(4,1)}), s8[4194304]{0:T(1024)(128)(4,1)S(1)}, s32[]{:S(2)}) async-start(s8[7274496]{0:T(1024)(128)(4,1)} %bitcast.147), calls=%async_computation.2 | async-start | bytes 8388608
  126.0 12.4 %slice-start.3 = ((s8[7274496]{0:T(1024)(128)(4,1)}), s8[3080192]{0:T(1024)(128)(4,1)S(1)}, s32[]{:S(2)}) async-start(s8[7274496]{0:T(1024)(128)(4,1)} %bitcast.147), calls=%async_computation.3 | async-start | bytes 6160384
  129.7 9.5 %copy-start.3 = (bf16[768,1152]{1,0:T(8,128)(2,1)}, bf16[768,1152]{1,0:T(8,128)(2,1)S(1)}, u32[]{:S(2)}) copy-start(bf16[768,1152]{1,0:T(8,128)(2,1)S(1)} %convolution_convert_fusion.1.qkv_ref.refs_12_) | copy-start | bytes 5308420
  138.3 1.9 copy-start.6
  138.4 1.9 copy-start.9
  139.2 2.9 collective-permute-start
  142.1 5.0 %slice-start = ((s8[7077888]{0:T(1024)(128)(4,1)}), s8[4194304]{0:T(1024)(128)(4,1)S(1)}, s32[]{:S(2)}) async-start(s8[7077888]{0:T(1024)(128)(4,1)} %bitcast.145), calls=%async_computation | async-start | bytes 8388608
  143.1 3.9 slice-start.1
  144.4 2.6 copy-start.21
  147.1 12.4 %copy-start.12 = (bf16[768,768]{1,0:T(8,128)(2,1)}, bf16[768,768]{1,0:T(8,128)(2,1)S(1)}, u32[]{:S(2)}) copy-start(bf16[768,768]{1,0:T(8,128)(2,1)S(1)} %get-tuple-element.83.refs_1_) | copy-start | bytes 3538948
  153.1 2.0 copy-start.14
  155.1 2.9 collective-permute-start.1
  161.4 15.6 %copy-start.13 = (bf16[768,768]{1,0:T(8,128)(2,1)}, bf16[768,768]{1,0:T(8,128)(2,1)S(1)}, u32[]{:S(2)}) copy-start(bf16[768,768]{1,0:T(8,128)(2,1)S(1)} %get-tuple-element.81.refs_2_) | copy-start | bytes 3538948
  163.1 9.5 %copy-start.4 = (bf16[768,1152]{1,0:T(8,128)(2,1)}, bf16[768,1152]{1,0:T(8,128)(2,1)S(1)}, u32[]{:S(2)}) copy-start(bf16[768,1152]{1,0:T(8,128)(2,1)S(1)} %convolution_convert_fusion.qkv_ref.refs_13_) | copy-start | bytes 5308420
  171.8 4.4 copy-start.7
  171.8 4.4 copy-start.10
  172.6 2.9 collective-permute-start.2
  178.9 13.4 %copy-start.11 = (bf16[768,768]{1,0:T(8,128)(2,1)}, bf16[768,768]{1,0:T(8,128)(2,1)S(1)}, u32[]{:S(2)}) copy-start(bf16[768,768]{1,0:T(8,128)(2,1)S(1)} %get-tuple-element.79.refs_3_) | copy-start | bytes 3538948
  184.7 2.0 copy-start.15
  186.7 4.2 collective-permute-start.3
  191.5 0.8 copy-start.24
  191.5 0.8 copy-start.25
  194.3 1.1 copy-start.17
  194.3 1.6 copy-start.23
  194.3 2.4 copy-start.30
  195.9 4.3 copy-start.18
  198.0 2.6 copy-start.32
  198.0 2.6 copy-start.33
  200.2 5.0 %copy-start.19 = (bf16[768,128]{1,0:T(8,128)(2,1)}, bf16[768,128]{1,0:T(8,128)(2,1)S(1)}, u32[]{:S(2)}) copy-start(bf16[768,128]{1,0:T(8,128)(2,1)S(1)} %fusion.51.refs_27_) | copy-start | bytes 589828
  200.2 4.0 copy-start.22
  459.1 1.8 copy-start.5
  460.7 2.1 copy-start.2

commit v2 on v1

--- a/solution.py
+++ b/solution.py
@@ -39,107 +39,7 @@
     r = lax.broadcasted_iota(jnp.int32, (rows, rows), 1)
     if which == 0:
         return (t // QUERY_LENGTH) == (r // QUERY_LENGTH)
-    return (t < bound) == (r < bound)
-
-
-def attention_kernel(bound_ref, qkv_ref, ctx_ref, lse_ref):
-    lane = lax.broadcasted_iota(jnp.int32, (1, 128), 1)
-    for which, (start, size) in enumerate(BLOCKS):
-        chunk = min(size, 256)
-        k = qkv_ref[start : start + size, 128:256]
-        v = qkv_ref[start : start + size, 256:384]
-        for at in range(start, start + size, chunk):
-            q = qkv_ref[at : at + chunk, 0:128]
-            total = None
-            for head in range(2):
-                mine = (lane < 64) if head == 0 else (lane >= 64)
-                qm = jnp.where(mine, q, jnp.zeros_like(q)) * BF(0.125)
-                vm = jnp.where(mine, v, jnp.zeros_like(v))
-                s = mm(k, qm, ((1,), (1,)))
-                if which != 1:
-                    s = jnp.where(block_mask(which, bound_ref[0], size), s, MASKED)
-                top = jnp.max(s, axis=0, keepdims=True)
-                e = jnp.exp(s - top)
-                weight = jnp.sum(e, axis=0, keepdims=True)
-                part = mm(vm, e.astype(BF), ((0,), (0,))) * (1.0 / weight)
-                total = part if total is None else total + part
-                lse_ref[0, head : head + 1, at : at + chunk] = top + jnp.log(weight)
-            ctx_ref[at : at + chunk, :] = total.T.astype(BF)
-
-
-def attention(qkv, bound):
-    return pl.pallas_call(
-        attention_kernel,
-        grid=(PAIRS,),
-        in_specs=[
-            pl.BlockSpec(memory_space=pltpu.SMEM),
-            pl.BlockSpec((ROWS, 384), lambda i: (0, i)),
-        ],
-        out_specs=[
-            pl.BlockSpec((ROWS, 128), lambda i: (0, i)),
-            pl.BlockSpec((1, 8, ROWS), lambda i: (i, 0, 0)),
-        ],
-        out_shape=[
-            jax.ShapeDtypeStruct((ROWS, HALF), BF),
-            jax.ShapeDtypeStruct((PAIRS, 8, ROWS), F32),
-        ],
-        compiler_params=pltpu.CompilerParams(vmem_limit_bytes=32 * 1024 * 1024),
-        cost_estimate=pl.CostEstimate(
-            flops=12 * 4 * 512 * 512 * 64, bytes_accessed=3000000, transcendentals=2000000
-        ),
-    )(bound, qkv)
-
-
-def attention_back_kernel(bound_ref, qkv_ref, dc_ref, lse_ref, out_ref):
-    lane = lax.broadcasted_iota(jnp.int32, (1, 128), 1)
-    for which, (start, size) in enumerate(BLOCKS):
-        chunk = min(size, 256)
-        k = qkv_ref[start : start + size, 128:256]
-        v = qkv_ref[start : start + size, 256:384]
-        dk = jnp.zeros((size, 128), F32)
-        dv = jnp.zeros((size, 128), F32)
-        for at in range(start, start + size, chunk):
-            q = qkv_ref[at : at + chunk, 0:128]
-            dc = dc_ref[at : at + chunk, :]
-            dq = None
-            for head in range(2):
-                mine = (lane < 64) if head == 0 else (lane >= 64)
-                qm = jnp.where(mine, q, jnp.zeros_like(q)) * BF(0.125)
-                dcm = jnp.where(mine, dc, jnp.zeros_like(dc))
-                km = jnp.where(mine, k, jnp.zeros_like(k))
-                s = mm(k, qm, ((1,), (1,)))
-                if which != 1:
-                    s = jnp.where(block_mask(which, bound_ref[0], size), s, MASKED)
-                p = jnp.exp(s - lse_ref[0, head : head + 1, at : at + chunk])
-                dp = mm(v, dcm, ((1,), (1,)))
-                inner = jnp.sum(p * dp, axis=0, keepdims=True)
-                ds = (p * (dp - inner)).astype(BF)
-                dv = dv + mm(p.astype(BF), dcm)
-                dk = dk + mm(ds, qm)
-                part = mm(km, ds, ((0,), (0,)))
-                dq = part if dq is None else dq + part
-            out_ref[at : at + chunk, 0:128] = (dq.T * 0.125).astype(BF)
-        out_ref[start : start + size, 128:256] = dk.astype(BF)
-        out_ref[start : start + size, 256:384] = dv.astype(BF)
-
-
-def attention_back(qkv, dc, lse, bound):
-    return pl.pallas_call(
-        attention_back_kernel,
-        grid=(PAIRS,),
-        in_specs=[
-            pl.BlockSpec(memory_space=pltpu.SMEM),
-            pl.BlockSpec((ROWS, 384), lambda i: (0, i)),
-            pl.BlockSpec((ROWS, 128), lambda i: (0, i)),
-            pl.BlockSpec((1, 8, ROWS), lambda i: (i, 0, 0)),
-        ],
-        out_specs=pl.BlockSpec((ROWS, 384), lambda i: (0, i)),
-        out_shape=jax.ShapeDtypeStruct((ROWS, 3 * HALF), BF),
-        compiler_params=pltpu.CompilerParams(vmem_limit_bytes=32 * 1024 * 1024),
-        cost_estimate=pl.CostEstimate(
-            flops=12 * 10 * 512 * 512 * 64, bytes_accessed=5000000, transcendentals=2000000
-        ),
-    )(bound, qkv, dc, lse)
+    return ((t.astype(F32) < bound).astype(F32) - (r.astype(F32) < bound).astype(F32)) == 0.0
 
 
 MESH = pl.DeviceIdType.MESH
@@ -183,34 +83,47 @@
         pl.semaphore_wait(barrier, 4)
 
 
-def fetch_kernel(
-    layers,
-    spread,
-    w_ref,
-    down_ref,
-    tail_ref,
-    vec_ref,
-    slices_ref,
-    ints_ref,
-    first_all,
-    rest_all,
-    vec_all,
-    parts_all,
-    ints_other,
-    wide,
-    out_stage,
-    down_stage,
-    first,
-    rest,
-    load_sem,
-    own_sem,
-    send_sem,
-    recv_sem,
-    z_send,
-    z_recv,
-    in_send,
-    in_recv,
-):
+def forward_kernel(layers, spread, queries_all, *refs):
+    w_ref, down_ref, tail_ref, vec_ref, slices_ref, ints_ref = refs[0:6]
+    first_out, rest_out, vec_out, h_out, xhat_out, scale_out, qkv_out, ctx_out = refs[6:14]
+    lse_out, act_out, slope_out, dw_out, tails_out, bound_out = refs[14:20]
+    (
+        first_all,
+        rest_all,
+        vec_all,
+        parts_all,
+        ints_other,
+        wide,
+        out_stage,
+        down_stage,
+        hs,
+        xhats,
+        scales,
+        qkvs,
+        ctxs,
+        lses,
+        acts,
+        slopes,
+        part_out,
+        part_in,
+        proj,
+        embedded,
+        unit,
+        length,
+        grad_unit,
+        grad_low,
+        tails,
+        load_sem,
+        send_sem,
+        recv_sem,
+        z_send,
+        z_recv,
+        in_send,
+        in_recv,
+        part_send,
+        part_recv,
+        save_sem,
+    ) = refs[20:]
     s, b, x, y, xy = neighbours()
     z, core = b // 2, b % 2
     micro = s // 2
@@ -245,13 +158,16 @@
         for copy in odd:
             copy.start()
 
+    first, rest = first_all.at[s], rest_all.at[s]
     tail = pltpu.make_async_copy(
         tail_ref, rest.at[pl.ds(FRONT, EXTRA), :], load_sem.at[13]
     )
+    own_vec = pltpu.make_async_copy(vec_ref, vec_all.at[s], load_sem.at[15])
+    own_vec.start()
     tail.start()
     greet(layers)
 
-    def feature(i, which, section, to):
+    def feature_copy(i, which, section, to):
         return pltpu.make_async_remote_copy(
             src_ref=slices_ref.at[which],
             dst_ref=parts_all.at[section],
@@ -281,12 +197,12 @@
     @pl.when(mine)
     def _():
         own_quarter.start()
-        feature(1, 1 - micro, s, y).start()
+        feature_copy(1, 1 - micro, s, y).start()
 
     @pl.when(jnp.logical_not(mine))
     def _():
-        feature(0, micro, s, x).start()
-        feature(2, 1 - micro, s, xy).start()
+        feature_copy(0, micro, s, x).start()
+        feature_copy(2, 1 - micro, s, xy).start()
 
     loads[0].wait()
 
@@ -385,12 +301,6 @@
     def late(n):
         direct(n, 1 if pieces[n][4] else 0).start()
 
-    own = [
-        pltpu.make_async_copy(first, first_all.at[s], own_sem.at[0]),
-        pltpu.make_async_copy(rest, rest_all.at[s], own_sem.at[1]),
-        pltpu.make_async_copy(vec_ref, vec_all.at[s], own_sem.at[2]),
-    ]
-
     z_width = D // layers if spread else 0
 
     def z_part(section, owner_z):
@@ -453,15 +363,13 @@
     queue_y = [n for n in by_y]
     for n in queue_x[:2] + queue_y[:2]:
         early(n)
-    for copy in own:
-        copy.start()
 
     @pl.when(mine)
     def _():
         own_quarter.wait()
         quarter_to_twin(3, s).start()
         for i, owner in enumerate((x, y, xy)):
-            feature(i, 0, owner, x).wait_recv()
+            feature_copy(i, 0, owner, x).wait_recv()
             quarter_to_twin(4 + i, owner).start()
     rounds = max(len(queue_x), len(queue_y))
     late_x, late_y = list(queue_y), list(queue_x)
@@ -496,7 +404,7 @@
     done = set()
     if spread:
         done = {(0, 1), (1, 0), (0, 2), (1, 2)}
-        while z_at < layers:
+        while z_at < layers - 1:
             z_step(z_at)
             z_at += 1
     for n in range(count):
@@ -504,80 +412,356 @@
             if kind == 2 or kind == (1 if pieces[n][4] else 0):
                 if (n, kind) not in done:
                     arrived(n, kind)
+    swap_ints.wait()
+    own_vec.wait()
+
+    @pl.when(jnp.logical_not(mine))
+    def _():
+        for i, owner in enumerate((s, x, y, xy)):
+            quarter_to_twin(3 + i, owner).wait_recv()
+
+    row = jnp.where(
+        mine, ints_ref[pl.ds(micro, 1), :].astype(F32), ints_other[pl.ds(micro, 1), :].astype(F32)
+    )
+    lane = lax.broadcasted_iota(jnp.int32, (1, 128), 1)
+
+    def entry(i):
+        return jnp.sum(jnp.where(lane == i, row, 0.0), axis=1, keepdims=True)
+
+    sizes = [entry(i) for i in range(PASSAGE_COUNT)]
+    is_long = [
+        (sizes[0] == float(PLEN)).astype(F32),
+        (sizes[1] == float(PLEN)).astype(F32),
+        (sizes[2] == float(PLEN)).astype(F32),
+    ]
+    bound = is_long[0] * sizes[1] + is_long[1] * sizes[2] + is_long[2] * sizes[0]
+    long_index = is_long[1] + 2.0 * is_long[2]
+
+    saves = []
+
+    def save(src, dst):
+        copy = pltpu.make_async_copy(src, dst, save_sem.at[len(saves)])
+        copy.start()
+        saves.append(copy)
+
+    save(vec_all, vec_out)
+    save(first_all, first_out)
+
+    def swap_copy(t, i):
+        rows = pl.ds(i * 256, 256)
+        return pltpu.make_async_remote_copy(
+            src_ref=part_out.at[rows, :],
+            dst_ref=part_in.at[t % 2, rows, :],
+            send_sem=part_send.at[t, i],
+            recv_sem=part_recv.at[t, i],
+            device_id=(s, twin),
+            device_id_type=MESH,
+        )
+
+    for i in range(6):
+        rows = slice(i * 128, (i + 1) * 128)
+        hs[0, rows, :] = jnp.concatenate([parts_all[f, rows, :] for f in range(4)], axis=1)
+    save(hs.at[0], h_out.at[0])
+
+    def norm_rows(t, i):
+        bias, gain, shift = vec_all[t, 0:1, :], vec_all[t, 1:2, :], vec_all[t, 2:3, :]
+        swap_copy(t, i).wait_recv()
+
+        def body(j, unused):
+            rows = pl.ds(pl.multiple_of(j * 128, 128), 128)
+            u = (
+                hs[t, rows, :].astype(F32)
+                + part_out[rows, :].astype(F32)
+                + part_in[t % 2, rows, :].astype(F32)
+                + bias
+            )
+            centered = u - jnp.mean(u, -1, keepdims=True)
+            scale = lax.rsqrt(jnp.mean(centered * centered, -1, keepdims=True) + NORM_EPSILON)
+            xhat = centered * scale
+            xhats[t, rows, :] = xhat.astype(BF)
+            scales[t, rows, :] = jnp.broadcast_to(scale, (128, 128))
+            hs[t + 1, rows, :] = (xhat * gain + shift).astype(BF)
+            return unused
+
+        lax.fori_loop(2 * i, 2 * i + 2, body, 0)
+
+    def save_norm(t):
+        save(xhats.at[t], xhat_out.at[t])
+        save(scales.at[t], scale_out.at[t])
+        if t < 3:
+            save(hs.at[t + 1], h_out.at[t + 1])
+
+    def attention_pair(l):
+        def pair(i, unused):
+            base = pl.multiple_of(i * 384, 128)
+            q_at = pl.ds(base, 128)
+            k_at = pl.ds(pl.multiple_of(base + 128, 128), 128)
+            v_at = pl.ds(pl.multiple_of(base + 256, 128), 128)
+            c_at = pl.ds(pl.multiple_of(i * 128, 128), 128)
+            for which, (begin, size) in enumerate(BLOCKS):
+                chunk = min(size, 256)
+                span = slice(begin, begin + size)
+                k = qkvs[l, span, k_at]
+                v = qkvs[l, span, v_at]
+                for at in range(begin, begin + size, chunk):
+                    rows = slice(at, at + chunk)
+                    q = qkvs[l, rows, q_at]
+                    total = None
+                    for head in range(2):
+                        own = (lane < 64) if head == 0 else (lane >= 64)
+                        qm = jnp.where(own, q, jnp.zeros_like(q)) * BF(0.125)
+                        vm = jnp.where(own, v, jnp.zeros_like(v))
+                        score = mm(k, qm, ((1,), (1,)))
+                        if which != 1:
+                            score = jnp.where(block_mask(which, bound, size), score, MASKED)
+                        top = jnp.max(score, axis=0, keepdims=True)
+                        e = jnp.exp(score - top)
+                        weight = jnp.sum(e, axis=0, keepdims=True)
+                        part = mm(vm, e.astype(BF), ((0,), (0,))) * (1.0 / weight)
+                        total = part if total is None else total + part
+                        lses[l, i, head : head + 1, rows] = top + jnp.log(weight)
+                    ctxs[l, rows, c_at] = total.T.astype(BF)
+            return unused
+
+        lax.fori_loop(0, PAIRS, pair, 0)
+
+    def attention_layer(l):
+        t = 2 * l
+        for i in range(3):
+            rows = slice(i * 256, (i + 1) * 256)
+            if t > 0:
+                norm_rows(t - 1, i)
+            qkvs[l, rows, :] = mm(hs[t, rows, :], first_all[t]).astype(BF)
+        if t > 0:
+            save_norm(t - 1)
+        save(qkvs.at[l], qkv_out.at[l])
+        attention_pair(l)
+        save(ctxs.at[l], ctx_out.at[l])
+        save(lses.at[l], lse_out.at[l])
+        for i in range(3):
+            rows = slice(i * 256, (i + 1) * 256)
+            if t > 0:
+                swap_copy(t - 1, i).wait_send()
+            part_out[rows, :] = mm(ctxs[l, rows, :], rest_all[t, 0:HALF, :]).astype(BF)
+            swap_copy(t, i).start()
+
+    def ffn_layer(l):
+        t = 2 * l + 1
+        for i in range(3):
+            rows = slice(i * 256, (i + 1) * 256)
+            norm_rows(t - 1, i)
+            x_rows = hs[t, rows, :]
+            for j in range(4):
+                columns = slice(j * HALF, (j + 1) * HALF)
+                if j < 3:
+                    value = mm(x_rows, first_all[t, :, columns])
+                else:
+                    value = mm(x_rows, rest_all[t, 0:HALF, :], ((1,), (1,)))
+                act, slope = gelu_and_slope(value)
+                acts[l, rows, columns] = act
+                slopes[l, rows, columns] = slope
+            swap_copy(t - 1, i).wait_send()
+            part = mm(acts[l, rows, 0:D], rest_all[2 * l, HALF:FRONT, :])
+            part = part + mm(acts[l, rows, D:], rest_all[2 * l + 1, HALF:FRONT, :])
+            part_out[rows, :] = part.astype(BF)
+            swap_copy(t, i).start()
+        save_norm(t - 1)
+        save(acts.at[l], act_out.at[l])
+        save(slopes.at[l], slope_out.at[l])
+
+    attention_layer(0)
+    if spread:
+        while z_at < layers:
+            z_step(z_at)
+            z_at += 1
+    save(rest_all, rest_out)
+    ffn_layer(0)
+    attention_layer(1)
+    ffn_layer(1)
+
+    for t in range(4):
+        proj[t * EXTRA : (t + 1) * EXTRA, :] = rest_all[t, FRONT : FRONT + EXTRA, :]
+    for i in range(3):
+        rows = slice(i * 256, (i + 1) * 256)
+        norm_rows(3, i)
+        w = mm(hs[4, rows, :], proj[...], ((1,), (1,)))
+        r = lax.rsqrt(jnp.sum(w * w, -1, keepdims=True) + NORM_EPSILON)
+        unit[rows, :] = w * r
+        length[rows, :] = jnp.broadcast_to(r, (256, 128))
+        embedded[rows, :] = (w * r).astype(BF)
+    save_norm(3)
+    queries, passages = embedded[0:QROWS, :], embedded[QROWS:, :]
+    logits = mm(queries, passages, ((1,), (1,))) * (1.0 / SOFTMAX_DIVISOR)
+    column = lax.broadcasted_iota(jnp.int32, (1, REST), 1).astype(F32)
+    token = lax.broadcasted_iota(jnp.int32, (QROWS, 1), 0)
+    before = column < bound
+    softs, shares = [], []
+    for p in range(3):
+        if p == 0:
+            score = logits[:, 0:PLEN]
+            top = jnp.max(score, -1, keepdims=True)
+            e = jnp.exp(score - top)
+        else:
+            score = logits[:, PLEN:]
+            inside = before if p == 1 else jnp.logical_not(before)
+            score = jnp.where(inside, score, MASKED)
+            top = jnp.max(score, -1, keepdims=True)
+            e = jnp.where(inside, jnp.exp(score - top), 0.0)
+        weight = jnp.sum(e, -1, keepdims=True)
+        softs.append(SOFTMAX_DIVISOR * (top + jnp.log(weight)))
+        shares.append(e * (1.0 / weight))
+    loss = jnp.zeros((1, 1), F32)
+    grad_softs = [jnp.zeros((QROWS, 1), F32) for p in range(3)]
+    for q in range(QUERY_COUNT):
+        mine_rows = (token // QUERY_LENGTH) == q
+        scores = [
+            SIMILARITY_SCALE * jnp.sum(jnp.where(mine_rows, soft, 0.0), 0, keepdims=True)
+            for soft in softs
+        ]
+        top = jnp.maximum(jnp.maximum(scores[0], scores[1]), scores[2])
+        es = [jnp.exp(score - top) for score in scores]
+        weight = es[0] + es[1] + es[2]
+        wanted = entry(PASSAGE_COUNT + q) - long_index
+        wanted = jnp.where(wanted < 0.0, wanted + 3.0, wanted)
+        chosen = [(wanted == float(p)).astype(F32) for p in range(3)]
+        picked = chosen[0] * scores[0] + chosen[1] * scores[1] + chosen[2] * scores[2]
+        loss = loss + top + jnp.log(weight) - picked
+        for p in range(3):
+            grad = (es[p] / weight - chosen[p]) * (SIMILARITY_SCALE / queries_all)
+            grad_softs[p] = jnp.where(mine_rows, grad, grad_softs[p])
+    grad_logits = jnp.concatenate(
+        [grad_softs[0] * shares[0], grad_softs[1] * shares[1] + grad_softs[2] * shares[2]], axis=1
+    ).astype(BF)
+    grad_unit[0:QROWS, :] = mm(grad_logits, passages)
+    grad_unit[QROWS:, :] = mm(grad_logits, queries, ((0,), (0,)))
+    for i in range(3):
+        rows = slice(i * 256, (i + 1) * 256)
+        n, dn = unit[rows, :], grad_unit[rows, :]
+        inner = jnp.sum(n * dn, -1, keepdims=True)
+        grad_low[rows, :] = (length[rows, :] * (dn - n * inner)).astype(BF)
+    save(grad_low, dw_out)
+    grad_proj = mm(grad_low[...], hs[4], ((0,), (0,)))
+    feature = lax.broadcasted_iota(jnp.int32, (16, D), 1)
+    line = lax.broadcasted_iota(jnp.int32, (16, D), 0)
+    head_rows = jnp.zeros((16, D), F32)
+    left = loss
+    for i, step in enumerate((8.0, 0.5, 2.0**-5, 2.0**-9, 2.0**-13, 2.0**-17)):
+        value = jnp.floor(left * (1.0 / step)) * step
+        left = left - value
+        head_rows = jnp.where((line == 3) & (feature == i), value, head_rows)
+    for t in range(4):
+        tails[t, 0:16, :] = head_rows.astype(BF)
+        tails[t, 16:TAIL, :] = grad_proj[t * EXTRA : (t + 1) * EXTRA, :].astype(BF)
+    save(tails, tails_out)
+    unit[0:8, :] = jnp.broadcast_to(bound, (8, 128))
+    save(unit.at[pl.ds(0, 8), :], bound_out)
+
+    for copy in saves:
+        copy.wait()
+    for i in range(3):
+        swap_copy(3, i).wait_send()
     for n in range(count):
         direct(n, 0).wait_send()
         direct(n, 1).wait_send()
         relay(n).wait_send()
     if spread:
         z_drain()
-    for copy in own:
-        copy.wait()
-    swap_ints.wait()
 
     @pl.when(mine)
     def _():
-        feature(1, 1 - micro, s, y).wait_send()
+        feature_copy(1, 1 - micro, s, y).wait_send()
         for i, owner in enumerate((s, x, y, xy)):
             quarter_to_twin(3 + i, owner).wait_send()
 
     @pl.when(jnp.logical_not(mine))
     def _():
-        feature(0, micro, s, x).wait_send()
-        feature(2, 1 - micro, s, xy).wait_send()
-        for i, owner in enumerate((s, x, y, xy)):
-            quarter_to_twin(3 + i, owner).wait_recv()
-
-
-def fetch_weights(w, down, tail, vec, slices, ints, layers):
+        feature_copy(0, micro, s, x).wait_send()
+        feature_copy(2, 1 - micro, s, xy).wait_send()
+
+
+def forward(w, down, tail, vec, slices, ints, layers, queries_all):
     spread = layers > 1 and D % (32 * layers) == 0
     anywhere = pl.BlockSpec(memory_space=pl.ANY)
+    inside = pl.BlockSpec(memory_space=pltpu.VMEM)
     pieces = 12 if not spread else 10
     steps = max(layers - 1, 1) if spread else 1
+    kept = [
+        ((4, D, FRONT), BF),
+        ((4, FRONT + EXTRA, D), BF),
+        ((4, 8, D), F32),
+        ((4, ROWS, D), BF),
+        ((4, ROWS, D), BF),
+        ((4, ROWS, 128), F32),
+        ((2, ROWS, FRONT), BF),
+        ((2, ROWS, HALF), BF),
+        ((2, PAIRS, 8, ROWS), F32),
+        ((2, ROWS, 2 * D), BF),
+        ((2, ROWS, 2 * D), BF),
+        ((ROWS, DIM), BF),
+        ((4, TAIL, D), BF),
+        ((8, 128), F32),
+    ]
     return pl.pallas_call(
-        partial(fetch_kernel, layers, spread),
-        in_specs=[anywhere] * 6,
-        out_specs=[anywhere] * 5,
-        out_shape=[
-            jax.ShapeDtypeStruct((4, D, FRONT), BF),
-            jax.ShapeDtypeStruct((4, FRONT + EXTRA, D), BF),
-            jax.ShapeDtypeStruct((4, 8, D), F32),
-            jax.ShapeDtypeStruct((4,) + slices.shape[1:], BF),
-            jax.ShapeDtypeStruct(ints.shape, jnp.int32),
-        ],
+        partial(forward_kernel, layers, spread, queries_all),
+        in_specs=[anywhere] * 3 + [inside, anywhere, inside],
+        out_specs=[anywhere] * len(kept),
+        out_shape=[jax.ShapeDtypeStruct(shape, kind) for shape, kind in kept],
         scratch_shapes=[
+            pltpu.VMEM((4, D, FRONT), BF),
+            pltpu.VMEM((4, FRONT + EXTRA, D), BF),
+            pltpu.VMEM((4, 8, D), F32),
+            pltpu.VMEM((4,) + slices.shape[1:], BF),
+            pltpu.VMEM(ints.shape, jnp.int32),
             pltpu.VMEM((D, 2 * D), F32),
             pltpu.VMEM((HALF, D), F32),
             pltpu.VMEM((D, D), F32),
-            pltpu.VMEM((D, FRONT), BF),
-            pltpu.VMEM((FRONT + EXTRA, D), BF),
-            pltpu.SemaphoreType.DMA((15,)),
-            pltpu.SemaphoreType.DMA((3,)),
+            pltpu.VMEM((5, ROWS, D), BF),
+            pltpu.VMEM((4, ROWS, D), BF),
+            pltpu.VMEM((4, ROWS, 128), F32),
+            pltpu.VMEM((2, ROWS, FRONT), BF),
+            pltpu.VMEM((2, ROWS, HALF), BF),
+            pltpu.VMEM((2, PAIRS, 8, ROWS), F32),
+            pltpu.VMEM((2, ROWS, 2 * D), BF),
+            pltpu.VMEM((2, ROWS, 2 * D), BF),
+            pltpu.VMEM((ROWS, D), BF),
+            pltpu.VMEM((2, ROWS, D), BF),
+            pltpu.VMEM((DIM, D), BF),
+            pltpu.VMEM((ROWS, DIM), BF),
+            pltpu.VMEM((ROWS, DIM), F32),
+            pltpu.VMEM((ROWS, DIM), F32),
+            pltpu.VMEM((ROWS, DIM), F32),
+            pltpu.VMEM((ROWS, DIM), BF),
+            pltpu.VMEM((4, TAIL, D), BF),
+            pltpu.SemaphoreType.DMA((16,)),
             pltpu.SemaphoreType.DMA((3, pieces)),
             pltpu.SemaphoreType.DMA((3, pieces)),
             pltpu.SemaphoreType.DMA((2, steps, 3)),
             pltpu.SemaphoreType.DMA((2, steps, 3)),
             pltpu.SemaphoreType.DMA((8,)),
             pltpu.SemaphoreType.DMA((8,)),
+            pltpu.SemaphoreType.DMA((4, 3)),
+            pltpu.SemaphoreType.DMA((4, 3)),
+            pltpu.SemaphoreType.DMA((32,)),
         ],
         compiler_params=pltpu.CompilerParams(
-            collective_id=1, has_side_effects=True, vmem_limit_bytes=40 * 1024 * 1024
+            collective_id=1, has_side_effects=True, vmem_limit_bytes=62 * 1024 * 1024
         ),
     )(w, down, tail, vec, slices, ints)
 
 
 TAIL = 48
 SIDE = HALF + TAIL
-STREAMS = ((D, FRONT, 32, True), (SIDE, D, 16, True), (D, D, 32, False))
+STREAMS = ((D, FRONT, 64, True), (SIDE, D, 48, False), (D, D, 64, True))
 CHUNKS = tuple(rows // step for rows, unused, step, unused2 in STREAMS)
+OFFSETS = (CHUNKS[2], CHUNKS[2] + CHUNKS[0], 0)
 ONE_LOW, ONE_HIGH, TWO, INWARD, BACK, TWIN = 0, 3, 6, 9, 12, 15
 
 
 def backward_kernel(layers, lags, *refs):
-    hs, xhats, scales = refs[0:4], refs[4:8], refs[8:12]
-    qkvs, ctxs, lses, acts, slopes = refs[12:14], refs[14:16], refs[16:18], refs[18:20], refs[20:22]
-    first_all, rest_all, tails, bound_ref, vec_ref, dw_ref = refs[22:28]
-    outs, out_back = refs[28:31], refs[31]
-    sums, ones, twos, ins, backs = refs[32:35], refs[35:38], refs[38:41], refs[41:44], refs[44:47]
+    first_all, rest_all, hs, xhats, scales, qkvs, ctxs, lses, acts, slopes, tails = refs[0:11]
+    bound_ref, vec_ref, dw_ref = refs[11:14]
+    outs, out_back = refs[14:17], refs[17]
+    sums, ones, twos, ins, backs = refs[18:21], refs[21:24], refs[24:27], refs[27:30], refs[30:33]
     (
         h_f,
         xhat_f,
@@ -610,7 +794,7 @@
         keep_sem,
         in_send,
         in_recv,
-    ) = refs[47:]
+    ) = refs[33:]
     s, b, x, y, xy = neighbours()
     z, core = b // 2, b % 2
     half = s // 2
@@ -630,10 +814,10 @@
     def loads_ffn(l):
         t = 2 * l + 1
         return [
-            load(hs[t], h_f, 0),
-            load(xhats[t], xhat_f, 1),
-            load(scales[t], scale_f, 2),
-            load(slopes[l], slope, 3),
+            load(hs.at[t], h_f, 0),
+            load(xhats.at[t], xhat_f, 1),
+            load(scales.at[t], scale_f, 2),
+            load(slopes.at[l], slope, 3),
             load(first_all.at[t], up_first, 4),
             load(rest_all.at[t, pl.ds(0, HALF), :], up_second, 5),
         ]
@@ -641,12 +825,12 @@
     def loads_attention(l):
         t = 2 * l
         return [
-            load(hs[t], h_a, 6),
-            load(xhats[t], xhat_a, 7),
-            load(scales[t], scale_a, 8),
-            load(qkvs[l], qkv, 9),
-            load(ctxs[l], ctx, 10),
-            load(lses[l], lse, 11),
+            load(hs.at[t], h_a, 6),
+            load(xhats.at[t], xhat_a, 7),
+            load(scales.at[t], scale_a, 8),
+            load(qkvs.at[l], qkv, 9),
+            load(ctxs.at[l], ctx, 10),
+            load(lses.at[l], lse, 11),
             load(first_all.at[t], att_first, 12),
             load(rest_all.at[t, pl.ds(0, HALF), :], att_second, 13),
         ]
@@ -656,7 +840,7 @@
         rows = pl.ds(HALF + (j % 2) * HALF, HALF)
         return (
             pltpu.make_async_copy(
-                acts[l].at[:, pl.ds(j * HALF, HALF)], act_ring.at[slot], ring_sem.at[0, slot]
+                acts.at[l, :, pl.ds(j * HALF, HALF)], act_ring.at[slot], ring_sem.at[0, slot]
             ),
             pltpu.make_async_copy(
                 rest_all.at[2 * l + j // 2, rows, :], down_ring.at[slot], ring_sem.at[1, slot]
@@ -748,22 +932,14 @@
             total = total + value.astype(F32)
         return total
 
-    def send_x_first(which, l, start_row, rows):
+    def send_block(which, t, start_row, rows):
         size = STREAMS[which][2]
-
-        def body(c, unused):
-            one(which, c, l).start()
-            return unused
-
-        lax.fori_loop(start_row // size, (start_row + rows) // size, body, 0)
-
-    def send_y_first(which, layer, p, start_row, rows):
-        size = STREAMS[which][2]
-
-        @pl.when(half != layer)
+        by_x = STREAMS[which][3]
+
+        @pl.when(parity != t % 2 if by_x else half != t // 2)
         def _():
             def body(c, unused):
-                one(which, c, p).start()
+                one(which, c, t // 2 if by_x else t % 2).start()
                 return unused
 
             lax.fori_loop(start_row // size, (start_row + rows) // size, body, 0)
@@ -830,7 +1006,7 @@
             sums[2][2 * l + j // 2, to : to + HALF, :] = mm(
                 act_ring[slot], low, ((0,), (0,))
             ).astype(BF)
-            send_y_first(2, l, j // 2, to, HALF)
+            send_block(2, 2 * l + j // 2, to, HALF)
             for i in range(3):
                 rows = slice(i * 256, (i + 1) * 256)
                 grad = mm(dy[rows, :], down_ring[slot], ((1,), (1,)))
@@ -878,7 +1054,7 @@
                     km = jnp.where(own, k, jnp.zeros_like(k))
                     score = mm(k, qm, ((1,), (1,)))
                     if which != 1:
-                        score = jnp.where(block_mask(which, bound_ref[0], size), score, MASKED)
+                        score = jnp.where(block_mask(which, bound_ref[0:1, 0:1], size), score, MASKED)
                     p = jnp.exp(score - lse[i, head : head + 1, rows])
                     dp = mm(v, dcm, ((1,), (1,)))
                     inner = jnp.sum(p * dp, axis=0, keepdims=True)
@@ -908,65 +1084,9 @@
             rows = slice(i * 256, (i + 1) * 256)
             sums[0][t, rows, :] = mm(h_a[:, rows], qkv[...], ((0,), (0,))).astype(BF)
 
-    def start_x_first(t):
-        l, p = t // 2, t % 2
-
-        @pl.when(parity != p)
-        def _():
-            for which in (1, 0):
-                send_x_first(which, l, 0, STREAMS[which][0])
-
-    wait(loads_ffn(1))
-    norm_back(3, grad_from_head, xhat_f, scale_f)
-    ffn_back(1)
-    start_x_first(3)
-    start(loads_ffn(0))
-    start(ring(0, 0))
-    start(ring(0, 1))
-    wait(loads_attention(1))
-    norm_back(2, grad_from(3), xhat_a, scale_a)
-    attention_grads(1)
-    start_x_first(2)
-    start(loads_attention(0))
-    wait(loads_ffn(0))
-    norm_back(1, grad_from(2), xhat_f, scale_f)
-    ffn_back(0)
-    start_x_first(1)
-    wait(loads_attention(0))
-    norm_back(0, grad_from(1), xhat_a, scale_a)
-    attention_grads(0)
-    start_x_first(0)
-
-    width = shares.shape[2]
-    for i in range(3):
-        swap_copy(0, i).wait_recv()
-
-        def body(j, unused):
-            rows = pl.ds(pl.multiple_of(j * 64, 64), 64)
-            total = plus(dy[rows, :], part_out[rows, :], part_in[0, rows, :])
-            for f in range(4):
-                shares[f, rows, :] = total[:, f * width : (f + 1) * width].astype(BF)
-            return unused
-
-        lax.fori_loop(4 * i, 4 * i + 4, body, 0)
-
-    def back_to(i, to):
-        return pltpu.make_async_remote_copy(
-            src_ref=shares.at[to],
-            dst_ref=out_back.at[i],
-            send_sem=in_send.at[i],
-            recv_sem=in_recv.at[i],
-            device_id=(to, b),
-            device_id_type=MESH,
-        )
-
-    own_share = pltpu.make_async_copy(shares.at[s], out_back.at[3], in_send.at[3])
-    own_share.start()
-
-    @pl.when(mine)
-    def _():
-        for i, to in enumerate((x, y, xy)):
-            back_to(i, to).start()
+    def send_sections(t):
+        for which in (1, 0):
+            send_block(which, t, 0, STREAMS[which][0])
 
     def came_one(which, chunk, l):
         one(which, chunk, l).wait_recv()
@@ -985,6 +1105,59 @@
         sums[which][t, rows, :] = plus(sums[which][t, rows, :], got).astype(BF)
         two(which, chunk).start()
 
+    wait(loads_ffn(1))
+    norm_back(3, grad_from_head, xhat_f, scale_f)
+    ffn_back(1)
+    send_sections(3)
+    start(loads_ffn(0))
+    start(ring(0, 0))
+    start(ring(0, 1))
+    wait(loads_attention(1))
+    norm_back(2, grad_from(3), xhat_a, scale_a)
+    attention_grads(1)
+    send_sections(2)
+    start(loads_attention(0))
+    wait(loads_ffn(0))
+    norm_back(1, grad_from(2), xhat_f, scale_f)
+    ffn_back(0)
+    send_sections(1)
+    wait(loads_attention(0))
+    norm_back(0, grad_from(1), xhat_a, scale_a)
+
+    attention_grads(0)
+    send_sections(0)
+
+    width = shares.shape[2]
+    for i in range(3):
+        swap_copy(0, i).wait_recv()
+
+        def body(j, unused):
+            rows = pl.ds(pl.multiple_of(j * 64, 64), 64)
+            total = plus(dy[rows, :], part_out[rows, :], part_in[0, rows, :])
+            for f in range(4):
+                shares[f, rows, :] = total[:, f * width : (f + 1) * width].astype(BF)
+            return unused
+
+        lax.fori_loop(4 * i, 4 * i + 4, body, 0)
+
+    def back_to(i, to):
+        return pltpu.make_async_remote_copy(
+            src_ref=shares.at[to],
+            dst_ref=out_back.at[i],
+            send_sem=in_send.at[i],
+            recv_sem=in_recv.at[i],
+            device_id=(to, b),
+            device_id_type=MESH,
+        )
+
+    own_share = pltpu.make_async_copy(shares.at[s], out_back.at[3], in_send.at[3])
+    own_share.start()
+
+    @pl.when(mine)
+    def _():
+        for i, to in enumerate((x, y, xy)):
+            back_to(i, to).start()
+
     def start_z(which, chunk):
         rows = rows_of(which, chunk)
         two(which, chunk).wait_recv()
@@ -1045,10 +1218,11 @@
 
     lag3 = lag_z + lag_step * depth
     lag5 = lag_z + lag_step * (middle + 1) + lag_step * (middle - depth)
-    slots = max(CHUNKS) + lag_z + (lag_step * (2 * middle + 1) if layers > 1 else 0)
-
-    def guarded(chunk, step):
+    slots = sum(CHUNKS) + lag_z + (lag_step * (2 * middle + 1) if layers > 1 else 0)
+
+    def guarded(position, step):
         for which, count in enumerate(CHUNKS):
+            chunk = position - OFFSETS[which]
 
             @pl.when((chunk >= 0) & (chunk < count))
             def _():
@@ -1088,7 +1262,7 @@
         guarded(k, drain)
         return unused
 
-    lax.fori_loop(0, max(CHUNKS), last, 0)
+    lax.fori_loop(0, sum(CHUNKS), last, 0)
     for i in range(3):
         swap_copy(0, i).wait_send()
     own_share.wait()
@@ -1105,15 +1279,14 @@
         back_to(2, xy).wait_recv()
 
 
-def backward(hs, xhats, scales, kept, first_all, rest_all, tails, bound, vec, dw, width, layers, lags=(1, 1)):
+def backward(first_all, rest_all, vec, kept, dw, tails, bound, width, layers, lags=(3, 2)):
     anywhere = pl.BlockSpec(memory_space=pl.ANY)
     inside = pl.BlockSpec(memory_space=pltpu.VMEM)
     shapes = [(rows, columns) for rows, columns, unused, unused2 in STREAMS]
     most = max(CHUNKS)
     return pl.pallas_call(
         partial(backward_kernel, layers, lags),
-        in_specs=[anywhere] * 25
-        + [pl.BlockSpec(memory_space=pltpu.SMEM), inside, inside],
+        in_specs=[anywhere] * 11 + [inside] * 3,
         out_specs=[anywhere] * 4,
         out_shape=[jax.ShapeDtypeStruct((2,) + shape, BF) for shape in shapes]
         + [jax.ShapeDtypeStruct((4, ROWS, width), BF)],
@@ -1156,7 +1329,7 @@
         compiler_params=pltpu.CompilerParams(
             collective_id=2, has_side_effects=True, vmem_limit_bytes=62 * 1024 * 1024
         ),
-    )(*hs, *xhats, *scales, *kept, first_all, rest_all, tails, bound, vec, dw)
+    )(first_all, rest_all, *kept, tails, bound, vec, dw)
 
 
 def assemble_kernel(first_ref, rest_ref, out_ref):
@@ -1199,32 +1372,10 @@
     )(first_sum, rest_sum)
 
 
-def layer_norm(residual, gain, shift):
-    row_mean = jnp.mean(residual, -1, keepdims=True)
-    centered = residual - row_mean
-    return (
-        centered * lax.rsqrt(jnp.mean(centered * centered, -1, keepdims=True) + NORM_EPSILON) * gain
-        + shift
-    )
-
-
-def normalize(projected):
-    return projected * lax.rsqrt(jnp.sum(projected * projected, -1, keepdims=True) + NORM_EPSILON)
-
-
 def gelu_and_slope(z):
     upper = 0.5 * (1.0 + lax.erf(z * 0.7071067811865476))
     density = jnp.exp(-0.5 * z * z) * 0.3989422804014327
     return (z * upper).astype(BF), (upper + z * density).astype(BF)
-
-
-def maxsim_loss(affinity, valid, positive):
-    logits = jnp.where(valid[None, :, :], affinity[:, None, :] / SOFTMAX_DIVISOR, MASKED)
-    soft = SOFTMAX_DIVISOR * jax.nn.logsumexp(logits, -1)
-    scores = jnp.sum(soft.reshape(QUERY_COUNT, QUERY_LENGTH, -1), 1) * SIMILARITY_SCALE
-    choose = jnp.arange(scores.shape[1], dtype=jnp.int32)[None, :] == positive[:, None]
-    picked = jnp.sum(jnp.where(choose, scores, 0.0), 1)
-    return jnp.sum(jax.nn.logsumexp(scores, -1) - picked)
 
 
 def on_device(
@@ -1281,102 +1432,18 @@
         ((0, 6), (0, 128 - PASSAGE_COUNT - QUERY_COUNT)),
     )
     vec = jnp.concatenate([out_bias, norm_gains, norm_shifts, jnp.zeros((5, D), F32)], 0)
-    first_all, rest_all, vectors, parts_all, ints_other = fetch_weights(
-        in_weight[0], down_weight, projection.T.astype(BF), vec, slices, ints, layers
+    first_all, rest_all, vectors, *kept, dw, tails, bound = forward(
+        in_weight[0],
+        down_weight,
+        projection.T.astype(BF),
+        vec,
+        slices,
+        ints,
+        layers,
+        queries_all,
     )
-    packs = [
-        (first_all[t], rest_all[t, :HALF], rest_all[t, HALF:FRONT]) for t in range(4)
-    ]
-    projector = jnp.concatenate([rest_all[t, FRONT:] for t in range(4)], 0).T
-    entry = jnp.concatenate([parts_all[f] for f in range(4)], 1)
-    ints = pick(jnp.where(mine, ints, ints_other), micro)
-    lengths = ints[:PASSAGE_COUNT]
-    chosen = ints[PASSAGE_COUNT : PASSAGE_COUNT + QUERY_COUNT]
-    long_index = jnp.where(lengths[0] == PLEN, 0, jnp.where(lengths[1] == PLEN, 1, 2))
-    after = (long_index + 1) % 3
-    bound = pick(lengths, after)
-    at = jnp.arange(PASSAGE_TOKENS, dtype=jnp.int32)
-    owner = jnp.where(at < PLEN, long_index, jnp.where(at < PLEN + bound, after, (after + 1) % 3))
-    valid = owner[None, :] == jnp.arange(PASSAGE_COUNT, dtype=jnp.int32)[:, None]
-    bound = bound.reshape(1)
-
-    def summed(part):
-        own = part.astype(BF)
-        return own.astype(F32) + other_core(own).astype(F32)
-
-    h = entry
-    hs, xhats, scales, kept = [], [], [], [[], [], [], [], []]
-    for t in range(4):
-        one, two, three = packs[t]
-        bias, gain, shift = vectors[t, 0], vectors[t, 1], vectors[t, 2]
-        if t % 2 == 0:
-            qkv = mm(h, one).astype(BF)
-            ctx, lse = attention(qkv, bound)
-            branch = summed(mm(ctx, two))
-            saved = (qkv, ctx, lse)
-        else:
-            down = jnp.concatenate([packs[t - 1][2], three], 0)
-            z = jnp.concatenate([mm(h, one), mm(h, two, ((1,), (1,)))], 1)
-            act, slope = gelu_and_slope(z)
-            branch = summed(mm(act, down))
-            saved = (None, None, None, act, slope)
-        residual = h.astype(F32) + branch + bias
-        centered = residual - jnp.mean(residual, -1, keepdims=True)
-        scale = lax.rsqrt(jnp.mean(centered * centered, -1, keepdims=True) + NORM_EPSILON)
-        xhat = centered * scale
-        hs.append(h)
-        xhats.append(xhat.astype(BF))
-        scales.append(jnp.broadcast_to(scale, (ROWS, 128)))
-        for i, value in enumerate(saved):
-            if value is not None:
-                kept[i].append(value)
-        h = (xhat * gain + shift).astype(BF)
-
-    projected = mm(h, projector)
-    normed, norm_pull = jax.vjp(normalize, projected)
-    embedded = normed.astype(BF)
-    affinity = mm(embedded[:QROWS], embedded[QROWS:], ((1,), (1,)))
-    loss, loss_pull = jax.vjp(partial(maxsim_loss, valid=valid, positive=chosen), affinity)
-    left, steps = loss, []
-    for unit in (8.0, 0.5, 2.0**-5, 2.0**-9, 2.0**-13, 2.0**-17):
-        steps.append(jnp.floor(left / unit) * unit)
-        left = left - steps[-1]
-    loss_row = jnp.pad(jnp.stack(steps), (0, D - len(steps)))
-    grad_sim = loss_pull(jnp.asarray(1.0 / queries_all, F32))[0].astype(BF)
-    grad_embedded = jnp.concatenate(
-        [mm(grad_sim, embedded[QROWS:]), mm(grad_sim, embedded[:QROWS], ((0,), (0,)))], 0
-    )
-    grad_projected = norm_pull(grad_embedded)[0].astype(BF)
-    grad_projector = mm(h, grad_projected, ((0,), (0,)))
-
-    columns = projection.shape[1]
-    tails = jnp.stack(
-        [
-            jnp.concatenate(
-                [
-                    jnp.zeros((3, D), F32),
-                    loss_row[None],
-                    jnp.zeros((12, D), F32),
-                    lax.slice_in_dim(grad_projector, t * columns, (t + 1) * columns, axis=1).T,
-                ],
-                0,
-            )
-            for t in range(4)
-        ]
-    ).astype(BF)
     first_sum, side_sum, down_sum, back = backward(
-        hs,
-        xhats,
-        scales,
-        sum(kept, []),
-        first_all,
-        rest_all,
-        tails,
-        bound,
-        vectors,
-        grad_projected,
-        inputs.shape[2],
-        layers,
+        first_all, rest_all, vectors, kept, dw, tails, bound, inputs.shape[2], layers
     )
     in_grad = assemble(first_sum, side_sum)
     down_grad = down_sum.reshape(2 * D, D).astype(F32)

time: 479 us -> 387 us (0.81)
  Pallas kernels: 380 us -> 353 us
  other arithmetic: 35.7 us -> 10 us
  matrix products: 17.4 us -> 0 us
  local copies, waits for them, and re-layouts: 22.3 us -> 11 us
  waiting for transfers between devices: 7.29 us -> 0 us
    pallas_call x1, Pallas kernels: 254 us -> 197 us  [backward(): pl.pallas_call(partial(backward_kernel, layers, lags), in_specs=[anywhere...]
    pallas_call x3 -> x1, Pallas kernels: 122 us -> 152 us  [forward(): pl.pallas_call(partial(forward_kernel, layers, spread, queries_all), in_s...]
    dot_general x15 -> x0, matrix products: 17.4 us -> none  [mm(): return lax.dot_general(a, b, (dims, ((), ())), preferred_element_type=F32)]
    convert_element_type x8 -> x0, other arithmetic: 15.7 us -> none  [the longest x2 6.86 us: gelu_and_slope(): return ((z * upper).astype(BF), (upper + z * density).astype(BF))]
    reduce_sum x13 -> x0, other arithmetic: 7.47 us -> none  [the longest x4 3.67 us: on_device(): jnp.mean(centered * centered, -1, keepdims=True) + NORM_EPSILON]
    ppermute x4 -> x0, waiting for transfers between devices: 7.29 us -> none  [other_core(): return lax.ppermute(value, 'batch', [(j, j ^ 1) for j in range(batches)])]
  transfers between devices with their start and end apart: 4 -> 0, of which waited for: 3 -> 0; matrix products, arithmetic and copies ran while one was open for 1% -> 0% of each run, Pallas kernels for 0% -> 0%
where the time goes in v2:
time: 387 us; the launch traced here: 384 us
  Pallas kernels  353 us (91%)
  local copies, waits for them, and re-layouts  11 us (3%)
  other arithmetic  10 us (3%)
  between operations  9.37 us (2%)
    pallas_call x1, Pallas kernels, backward(): pl.pallas_call(partial(backward_kernel, layers, lags), in_specs=[anywhere...  197 us
    pallas_call x1, Pallas kernels, forward(): pl.pallas_call(partial(forward_kernel, layers, spread, queries_all), in_s...  152 us

profile of v2, /device:TPU:0, one launch (start us, length us, event | category | flops | bytes accessed | tf_op | source)
XLA Modules:
  0.0 383.8 jit_solution(7060527795715719392)
XLA Ops:
  0.6 1.3 fusion.7
  5.2 0.9 fusion.5
  6.1 0.1 copy.29
  6.2 0.0 copy-start.3
  6.2 0.0 copy-start.5
  6.2 0.0 copy-start.6
  6.2 0.0 copy-start.7
  6.3 0.0 copy-start.4
  6.3 0.0 copy-start.8
  6.3 1.2 fusion.6
  7.4 0.2 copy.28
  7.6 0.6 fusion.2
  11.5 0.1 copy.26
  11.6 0.2 copy.25
  11.8 0.6 fusion.3
  12.4 0.1 copy.24
  12.5 0.1 copy.27
  12.6 0.1 maximum_bitcast_fusion.2
  12.8 1.0 pad_maximum_fusion.1.refs_4_
  13.8 0.0 copy-done.3
  13.8 0.6 convert_bitcast_fusion.refs_2_
  14.4 0.1 pad.30.clone
  14.5 0.0 copy-done.5
  14.5 0.0 copy-done.6
  14.5 0.0 copy-done.7
  14.5 0.7 maximum_maximum_fusion.refs_3_
  15.2 0.0 copy-done.4
  15.2 0.0 copy-done.8
  15.2 0.1 pad_add_fusion
  15.3 0.6 pad.4.refs_5_
  15.9 151.7 %shard_map.152 = (bf16[4,768,1152]{2,1,0:T(8,128)(2,1)}, bf16[4,1184,768]{2,1,0:T(8,128)(2,1)}, f32[4,8,768]{2,1,0:T(8,128)}, bf16[4,768,768]{2,1,0:T(8,128)(2,1...) custom-call(f32[768,3072]{1,0:T(8,128)} %bitcast.51, ...), custom_call_target="tpu_custom_call" | custom-call | tf_op jit(solution)/shard_map/pallas_call | solution.py:704
  167.5 197.2 %shard_map.153 = (bf16[2,768,1152]{2,1,0:T(8,128)(2,1)}, bf16[2,432,768]{2,1,0:T(8,128)(2,1)}, bf16[2,768,768]{2,1,0:T(8,128)(2,1)}, bf16[4,768,192]{2,1,0:T(8,128)(2,1)}) custom-call(bf16[4,768,1152]{2,1,0:T(8,128)(2,1)} %get-tuple-element.26.refs_0_, bf16[4,1184,768]{2,1,0:T(8,128)(2,1)} %get-tuple-element.27.refs_1_, ...), custom_call_target="tpu_custom_call" | custom-call | tf_op jit(solution)/shard_map/pallas_call | solution.py:1287
  364.7 0.0 copy-start
  364.7 2.0 copy-done
  366.7 0.0 copy-start.1
  366.7 1.3 copy-done.1
  368.1 0.0 copy-start.2
  368.1 4.6 %shard_map.154 = f32[768,3072]{1,0:T(8,128)} custom-call(bf16[2,768,1152]{2,1,0:T(8,128)(2,1)S(1)} %copy-done, bf16[2,432,768]{2,1,0:T(8,128)(2,1)S(1)} %copy-done.1), custom_call_target="tpu_custom_call" | custom-call | tf_op jit(solution)/shard_map/pallas_call | solution.py:1362
  372.6 0.0 copy-done.2
  372.6 0.1 select_convert_fusion.1
  372.9 0.1 fusion.1
  373.0 0.1 maximum_bitcast_fusion
  373.1 0.1 fusion
  373.2 0.1 maximum_bitcast_fusion.1
  373.3 0.1 pad_maximum_fusion
  373.4 1.5 copy.23
  374.9 4.2 %bitcast_convert_fusion = f32[1536,768]{1,0:T(8,128)} fusion(bf16[2,768,768]{2,1,0:T(8,128)(2,1)} %get-tuple-element.43), kind=kLoop, calls=%fused_computation | loop fusion | flops 1179648 | bytes 7077888 | tf_op jit(solution)/shard_map/convert_element_type | solution.py:1449
  379.1 0.9 slice_convert_fusion
  380.0 0.6 slice_bitcast_fusion.6
  380.6 0.6 slice_bitcast_fusion.7
  381.2 0.6 slice_reduce_fusion
  (5 shorter events, 0.1 us)
Async XLA Ops:
  6.2 7.6 %copy-start.3 = (f32[768,32]{0,1:T(8,128)S(1)}, f32[768,32]{0,1:T(8,128)}, u32[]{:S(2)}) copy-start(f32[768,32]{0,1:T(8,128)} %param.15) | copy-start | bytes 294916
  6.2 8.3 %copy-start.5 = (f32[1,768]{1,0:T(1,128)S(1)}, f32[1,768]{1,0:T(1,128)}, u32[]{:S(2)}) copy-start(f32[1,768]{1,0:T(1,128)} %param.14) | copy-start | bytes 9220
  6.2 8.3 %copy-start.6 = (f32[1,768]{1,0:T(1,128)S(1)}, f32[1,768]{1,0:T(1,128)}, u32[]{:S(2)}) copy-start(f32[1,768]{1,0:T(1,128)} %param.13) | copy-start | bytes 9220
  6.2 8.3 %copy-start.7 = (f32[1,768]{1,0:T(1,128)S(1)}, f32[1,768]{1,0:T(1,128)}, u32[]{:S(2)}) copy-start(f32[1,768]{1,0:T(1,128)} %param.12) | copy-start | bytes 9220
  6.3 8.9 %copy-start.4 = (s32[2,1,3]{2,1,0:T(1,128)S(1)}, s32[2,1,3]{2,1,0:T(1,128)}, u32[]{:S(2)}) copy-start(s32[2,1,3]{2,1,0:T(1,128)} %param.16) | copy-start | bytes 76
  6.3 8.9 %copy-start.8 = (s32[2,4]{1,0:T(2,128)S(1)}, s32[2,4]{1,0:T(2,128)}, u32[]{:S(2)}) copy-start(s32[2,4]{1,0:T(2,128)} %param.17) | copy-start | bytes 100
  364.7 2.0 copy-start
  366.7 1.3 copy-start.1
  368.1 4.6 %copy-start.2 = (bf16[4,768,192]{2,1,0:T(8,128)(2,1)S(1)}, bf16[4,768,192]{2,1,0:T(8,128)(2,1)}, u32[]{:S(2)}) copy-start(bf16[4,768,192]{2,1,0:T(8,128)(2,1)} %get-tuple-element.41) | copy-start | bytes 3538948
